TPU v7x, 32 devices: a whole 2x2x4 slice. The times are simulated.
32 devices in a mesh: section: 2 (over core), dp: 4 (over z), expert: 4 (over y, x).
Axes of the slice: x: 2, y: 2, z: 4, core: 2. Of those that a mesh axis runs over, the one named last changes fastest.
Arguments:
- layer_input: bfloat16 [2, 1024, 1024], P(None, ('dp', 'expert')), may hold values from -6 to 6
- cotangent: bfloat16 [2, 1024, 1024], P(None, ('dp', 'expert')), may hold values from -6 to 6
- positions: int32 [2, 1024], P(None, ('dp', 'expert')), may hold values from 0 to 63, as said below
- routes: int32 [2, 2, 1024, 8], P('section', None, ('dp', 'expert')), may hold values from 0 to 31, all different within a row; in each aligned block of 64 rows (0 to 63, 64 to 127, ..., all dimensions but the last counted through in order) at most 32 rows name the same one
- gain_one: float32 [2, 1024], P('section'), may hold values from 0.5 to 1.5
- attn_in: bfloat16 [2, 1024, 2048], P('section', 'dp'), may hold values from -0.1875 to 0.1875
- attn_out: bfloat16 [2, 1024, 1024], P('section', 'dp'), may hold values from -1 to 1
- gain_two: float32 [2, 1024], P('section'), may hold values from 0.5 to 1.5
- router: bfloat16 [2, 1024, 32], P('section'), may hold values from -0.09375 to 0.09375
- experts_in: bfloat16 [2, 32, 1024, 1024], P('section', 'expert'), may hold values from -0.1875 to 0.1875
- experts_out: bfloat16 [2, 32, 512, 1024], P('section', 'expert'), may hold values from -1.5 to 1.5
Outputs:
- hidden: bfloat16 [2, 2, 1024, 1024], P('section', None, ('dp', 'expert'))
- input_grad: bfloat16 [2, 2, 1024, 1024], P('section', None, ('dp', 'expert'))
- grad_gain_one: float32 [2, 1024], P('section')
- grad_attn_in: float32 [2, 1024, 2048], P('section', ('dp', 'expert'))
- grad_attn_out: float32 [2, 1024, 1024], P('section', ('dp', 'expert'))
- grad_gain_two: float32 [2, 1024], P('section')
- grad_router: float32 [2, 1024, 32], P('section')
- grad_experts_in: float32 [2, 32, 1024, 1024], P('section', 'expert', 'dp')
- grad_experts_out: float32 [2, 32, 512, 1024], P('section', 'expert', 'dp')
Inputs may be any that keep to these rules, and one draw needn't show every extreme that they name: `routes`: each token names 8 different experts of 32. Among the 64 tokens of one sequence in one layer, no expert is named more than 32 times, and in some sequences one is named exactly 32 times. `positions`: within each sequence of 64 tokens a position is 0 at the first token and at the start of each packed document, and one more than the previous token's elsewhere.
All inputs are finite; a program needn't handle non-finite values.
Results may differ from a plain program's by a relative error of at most 0.025.
Values may be sent and summed in bfloat16 or wider, within the bound.
A program may use at most 320 MiB of HBM per device.

v0:
```python
import jax
import jax.numpy as jnp
from jax import lax
from jax.sharding import PartitionSpec as P

MODEL_WIDTH = 1024
QUERY_HEADS = 16
KEY_VALUE_HEADS = 8
HEAD_SIZE = 64
FF = 512
EXPERTS = 32
TOPK = 8
CAP = 32


epsilon = 1e-06
rotary_base = 10000.0


def shifted(shard, axis, by):
    length = lax.axis_size(axis)
    pairs = [(i, i + by) for i in range(length) if 0 <= i + by < length]
    return lax.ppermute(shard, axis, pairs)


def rms_scale(values):
    return lax.rsqrt(jnp.mean(values * values, axis=-1, keepdims=True) + epsilon)


def norm_back(grad_normed, inputs, scale):
    return scale * grad_normed - inputs * (scale * scale * scale) * jnp.mean(
        grad_normed * inputs, axis=-1, keepdims=True
    )


def rotary_tables(place_now):
    half_size = HEAD_SIZE // 2
    frequency = jnp.power(
        rotary_base, -(jnp.arange(half_size, dtype=jnp.float32) * (2.0 / HEAD_SIZE))
    )
    angles = place_now.astype(jnp.float32)[:, None] * frequency[None, :]
    cosine_table = jnp.concatenate([jnp.cos(angles), jnp.cos(angles)], axis=-1)[:, None, :]
    sine_table = jnp.concatenate([jnp.sin(angles), jnp.sin(angles)], axis=-1)[:, None, :]
    return (cosine_table, sine_table)


def apply_rotary(values, cosine_table, sine_table):
    half_size = HEAD_SIZE // 2
    turned = jnp.concatenate([-values[..., half_size:], values[..., :half_size]], axis=-1)
    return values * cosine_table + turned * sine_table


def invert_rotary(incoming_grad, cosine_table, sine_table):
    half_size = HEAD_SIZE // 2
    times_sine = incoming_grad * sine_table
    turned_back = jnp.concatenate(
        [times_sine[..., half_size:], -times_sine[..., :half_size]], axis=-1
    )
    return incoming_grad * cosine_table + turned_back


def split_heads(projection_output, cosine_table, sine_table):
    sequence_length = projection_output.shape[0]
    query_width = QUERY_HEADS * HEAD_SIZE
    key_width = KEY_VALUE_HEADS * HEAD_SIZE
    query_rows = apply_rotary(
        projection_output[:, :query_width].reshape(sequence_length, QUERY_HEADS, HEAD_SIZE),
        cosine_table,
        sine_table,
    ).astype(jnp.bfloat16)
    rotated_keys = apply_rotary(
        projection_output[:, query_width : query_width + key_width].reshape(
            sequence_length, KEY_VALUE_HEADS, HEAD_SIZE
        ),
        cosine_table,
        sine_table,
    ).astype(jnp.bfloat16)
    value_rows_full = (
        projection_output[:, query_width + key_width :]
        .reshape(sequence_length, KEY_VALUE_HEADS, HEAD_SIZE)
        .astype(jnp.bfloat16)
    )
    return (query_rows, rotated_keys, value_rows_full)


def join_heads(
    gradient_query_rows, gradient_key_rows, gradient_value_rows, cosine_table, sine_table
):
    sequence_length = gradient_query_rows.shape[0]
    return jnp.concatenate(
        [
            invert_rotary(gradient_query_rows, cosine_table, sine_table).reshape(
                sequence_length, QUERY_HEADS * HEAD_SIZE
            ),
            invert_rotary(gradient_key_rows, cosine_table, sine_table).reshape(
                sequence_length, KEY_VALUE_HEADS * HEAD_SIZE
            ),
            gradient_value_rows.reshape(sequence_length, KEY_VALUE_HEADS * HEAD_SIZE),
        ],
        axis=-1,
    ).astype(jnp.bfloat16)


def attention_scores(query_rows, rotated_keys):
    sequence_length = query_rows.shape[0]
    head_grouped = query_rows.reshape(
        sequence_length, KEY_VALUE_HEADS, QUERY_HEADS // KEY_VALUE_HEADS, HEAD_SIZE
    )
    scores = jnp.einsum(
        "qkgd,skd->kgqs", head_grouped, rotated_keys, preferred_element_type=jnp.float32
    ) * HEAD_SIZE ** (-0.5)
    allowed = jnp.arange(sequence_length)[:, None] >= jnp.arange(sequence_length)[None, :]
    return jnp.where(allowed, scores, -1e30)


def attention_forward(query_rows, rotated_keys, value_rows_full):
    sequence_length = query_rows.shape[0]
    scores = attention_scores(query_rows, rotated_keys)
    row_top = jnp.max(scores, axis=-1, keepdims=True)
    logarithm_total = row_top + jnp.log(jnp.sum(jnp.exp(scores - row_top), axis=-1, keepdims=True))
    weights = jnp.exp(scores - logarithm_total).astype(jnp.bfloat16)
    attention_result = jnp.einsum(
        "kgqs,skd->qkgd", weights, value_rows_full, preferred_element_type=jnp.float32
    )
    return (
        attention_result.reshape(sequence_length, QUERY_HEADS * HEAD_SIZE).astype(jnp.bfloat16),
        logarithm_total,
    )


def attention_backward(
    query_rows,
    rotated_keys,
    value_rows_full,
    attention_result,
    logarithm_total,
    gradient_attention_result,
):
    sequence_length = query_rows.shape[0]
    query_groups = QUERY_HEADS // KEY_VALUE_HEADS
    scores = attention_scores(query_rows, rotated_keys)
    probabilities = jnp.exp(scores - logarithm_total)
    gradient_quad = gradient_attention_result.reshape(
        sequence_length, KEY_VALUE_HEADS, query_groups, HEAD_SIZE
    )
    attention_quad = attention_result.reshape(
        sequence_length, KEY_VALUE_HEADS, query_groups, HEAD_SIZE
    )
    row_delta = jnp.einsum(
        "qkgd,qkgd->kgq", gradient_quad, attention_quad, preferred_element_type=jnp.float32
    )
    grad_probs = jnp.einsum(
        "qkgd,skd->kgqs", gradient_quad, value_rows_full, preferred_element_type=jnp.float32
    )
    grad_scores = (probabilities * (grad_probs - row_delta[..., None])).astype(jnp.bfloat16)
    head_grouped = query_rows.reshape(sequence_length, KEY_VALUE_HEADS, query_groups, HEAD_SIZE)
    gradient_query_rows = jnp.einsum(
        "kgqs,skd->qkgd", grad_scores, rotated_keys, preferred_element_type=jnp.float32
    ).reshape(sequence_length, QUERY_HEADS, HEAD_SIZE) * HEAD_SIZE ** (-0.5)
    gradient_key_rows = jnp.einsum(
        "kgqs,qkgd->skd", grad_scores, head_grouped, preferred_element_type=jnp.float32
    ) * HEAD_SIZE ** (-0.5)
    gradient_value_rows = jnp.einsum(
        "kgqs,qkgd->skd",
        probabilities.astype(jnp.bfloat16),
        gradient_quad,
        preferred_element_type=jnp.float32,
    )
    return (gradient_query_rows, gradient_key_rows, gradient_value_rows)


def expert_forward(arrived, expert_in, expert_out):
    hidden_pair = jnp.einsum("erd,edf->erf", arrived, expert_in, preferred_element_type=jnp.float32)
    gate_part = hidden_pair[..., :FF]
    up_part = hidden_pair[..., FF:]
    activated = (gate_part * jax.nn.sigmoid(gate_part) * up_part).astype(jnp.bfloat16)
    return jnp.einsum(
        "erf,efd->erd", activated, expert_out, preferred_element_type=jnp.float32
    ).astype(jnp.bfloat16)


def expert_backward(arrived, arrived_grads, expert_in, expert_out):
    hidden_pair = jnp.einsum("erd,edf->erf", arrived, expert_in, preferred_element_type=jnp.float32)
    gate_part = hidden_pair[..., :FF]
    up_part = hidden_pair[..., FF:]
    sigmoid_gate = jax.nn.sigmoid(gate_part)
    silu_gate = gate_part * sigmoid_gate
    activated = (silu_gate * up_part).astype(jnp.bfloat16)
    grad_act = jnp.einsum(
        "erd,efd->erf", arrived_grads, expert_out, preferred_element_type=jnp.float32
    )
    delta_out = jnp.einsum(
        "erf,erd->efd", activated, arrived_grads, preferred_element_type=jnp.float32
    )
    grad_gate = grad_act * up_part * sigmoid_gate * (1.0 + gate_part * (1.0 - sigmoid_gate))
    grad_up = grad_act * silu_gate
    grad_pair = jnp.concatenate([grad_gate, grad_up], axis=-1).astype(jnp.bfloat16)
    delta_in = jnp.einsum("erd,erf->edf", arrived, grad_pair, preferred_element_type=jnp.float32)
    back_rows = jnp.einsum(
        "erf,edf->erd", grad_pair, expert_in, preferred_element_type=jnp.float32
    ).astype(jnp.bfloat16)
    return (back_rows, delta_in, delta_out)


def route_slots(choices, experts_here, owners):
    flat_rows = choices.reshape(-1)
    row_total = flat_rows.shape[0]
    onehot_table = (flat_rows[:, None] == jnp.arange(EXPERTS, dtype=jnp.int32)[None, :]).astype(
        jnp.float32
    )
    row_iota = jnp.arange(row_total, dtype=jnp.int32)
    lower_ones = (row_iota[:, None] >= row_iota[None, :]).astype(jnp.float32)
    running = jnp.dot(
        lower_ones,
        onehot_table,
        precision=lax.Precision.HIGHEST,
        preferred_element_type=jnp.float32,
    )
    slot_rank = jnp.sum((running - 1.0) * onehot_table, axis=1).astype(jnp.int32)
    owner_local = flat_rows % experts_here
    slot_column = flat_rows // experts_here * CAP + slot_rank
    flat_slot = owner_local * (owners * CAP) + slot_column
    slot_total = experts_here * owners * CAP
    placement = (jnp.arange(slot_total, dtype=jnp.int32)[:, None] == flat_slot[None, :]).astype(
        jnp.bfloat16
    )
    table_three = onehot_table.reshape(choices.shape[0], TOPK, EXPERTS)
    return (table_three, placement)


def layer_forward(entering, choices, place_now, params):
    gain_first, weights_in, weights_out, gain_second, router_weights, expert_in, expert_out = params
    sequence_length = entering.shape[0]
    experts_here = expert_in.shape[0]
    owners = lax.axis_size("expert")
    residual = entering.astype(jnp.float32)
    scale_first = rms_scale(residual)
    normed_first = (residual * scale_first * gain_first).astype(jnp.bfloat16)
    projection_output = jnp.dot(normed_first, weights_in, preferred_element_type=jnp.float32)
    cosine_table, sine_table = rotary_tables(place_now)
    query_rows, rotated_keys, value_rows_full = split_heads(
        projection_output, cosine_table, sine_table
    )
    attention_result, logarithm_total = attention_forward(query_rows, rotated_keys, value_rows_full)
    middle = residual + jnp.dot(attention_result, weights_out, preferred_element_type=jnp.float32)
    scale_second = rms_scale(middle)
    normed_second = (middle * scale_second * gain_second).astype(jnp.bfloat16)
    logits = jnp.dot(normed_second, router_weights, preferred_element_type=jnp.float32)
    table_three, placement = route_slots(choices, experts_here, owners)
    picked = jnp.sum(table_three * logits[:, None, :], axis=-1)
    gate_probs = jax.nn.softmax(picked, axis=-1)
    slot_total = placement.shape[0]
    token_place = jnp.sum(
        placement.reshape(slot_total, sequence_length, TOPK), axis=2, dtype=jnp.float32
    ).astype(jnp.bfloat16)
    outgoing = (
        jnp.dot(token_place, normed_second, preferred_element_type=jnp.float32)
        .astype(jnp.bfloat16)
        .reshape(experts_here, owners * CAP, MODEL_WIDTH)
    )
    arrived = lax.all_to_all(outgoing, "expert", split_axis=1, concat_axis=1, tiled=True)
    produced = expert_forward(arrived, expert_in, expert_out)
    returned = lax.all_to_all(produced, "expert", split_axis=1, concat_axis=1, tiled=True)
    picked_rows = jnp.dot(
        placement.T, returned.reshape(slot_total, MODEL_WIDTH), preferred_element_type=jnp.float32
    ).astype(jnp.bfloat16)
    mixture = jnp.einsum(
        "skd,sk->sd",
        picked_rows.reshape(sequence_length, TOPK, MODEL_WIDTH),
        gate_probs,
        preferred_element_type=jnp.float32,
    )
    leaving = (middle + mixture).astype(jnp.bfloat16)
    kept_state = (
        residual,
        scale_first,
        normed_first,
        query_rows,
        rotated_keys,
        value_rows_full,
        attention_result,
        logarithm_total,
        middle,
        scale_second,
        normed_second,
        table_three,
        gate_probs,
        placement,
        arrived,
        picked_rows,
        cosine_table,
        sine_table,
    )
    return (leaving, kept_state)


def layer_backward(kept_state, arriving, params):
    (
        residual,
        scale_first,
        normed_first,
        query_rows,
        rotated_keys,
        value_rows_full,
        attention_result,
        logarithm_total,
        middle,
        scale_second,
        normed_second,
        table_three,
        gate_probs,
        placement,
        arrived,
        picked_rows,
        cosine_table,
        sine_table,
    ) = kept_state
    gain_first, weights_in, weights_out, gain_second, router_weights, expert_in, expert_out = params
    sequence_length = arriving.shape[0]
    experts_here = expert_in.shape[0]
    owners = lax.axis_size("expert")
    slot_total = placement.shape[0]
    upstream = arriving.astype(jnp.float32)
    row_three = picked_rows.reshape(sequence_length, TOPK, MODEL_WIDTH)
    grad_gates = jnp.einsum("skd,sd->sk", row_three, upstream, preferred_element_type=jnp.float32)
    row_grads = (
        (gate_probs[:, :, None] * upstream[:, None, :])
        .astype(jnp.bfloat16)
        .reshape(sequence_length * TOPK, MODEL_WIDTH)
    )
    outgoing = (
        jnp.dot(placement, row_grads, preferred_element_type=jnp.float32)
        .astype(jnp.bfloat16)
        .reshape(experts_here, owners * CAP, MODEL_WIDTH)
    )
    arrived_grads = lax.all_to_all(outgoing, "expert", split_axis=1, concat_axis=1, tiled=True)
    back_rows, delta_in, delta_out = expert_backward(arrived, arrived_grads, expert_in, expert_out)
    returned_grads = lax.all_to_all(back_rows, "expert", split_axis=1, concat_axis=1, tiled=True)
    gathered_back = jnp.dot(
        placement.T,
        returned_grads.reshape(slot_total, MODEL_WIDTH),
        preferred_element_type=jnp.float32,
    )
    grad_second = jnp.sum(gathered_back.reshape(sequence_length, TOPK, MODEL_WIDTH), axis=1)
    grad_picked = gate_probs * (
        grad_gates - jnp.sum(gate_probs * grad_gates, axis=-1, keepdims=True)
    )
    grad_logits = jnp.sum(table_three * grad_picked[:, :, None], axis=1).astype(jnp.bfloat16)
    delta_router = jnp.dot(normed_second.T, grad_logits, preferred_element_type=jnp.float32)
    grad_second = grad_second + jnp.dot(
        grad_logits, router_weights.T, preferred_element_type=jnp.float32
    )
    delta_gain_second = jnp.sum(grad_second * middle * scale_second, axis=0)
    grad_middle = upstream + norm_back(grad_second * gain_second, middle, scale_second)
    grad_middle_low = grad_middle.astype(jnp.bfloat16)
    delta_attn_out = jnp.dot(
        attention_result.T, grad_middle_low, preferred_element_type=jnp.float32
    )
    gradient_attention_result = jnp.dot(
        grad_middle_low, weights_out.T, preferred_element_type=jnp.float32
    ).astype(jnp.bfloat16)
    gradient_query_rows, gradient_key_rows, gradient_value_rows = attention_backward(
        query_rows,
        rotated_keys,
        value_rows_full,
        attention_result,
        logarithm_total,
        gradient_attention_result,
    )
    gradient_projection_output = join_heads(
        gradient_query_rows, gradient_key_rows, gradient_value_rows, cosine_table, sine_table
    )
    delta_attn_in = jnp.dot(
        normed_first.T, gradient_projection_output, preferred_element_type=jnp.float32
    )
    grad_first = jnp.dot(
        gradient_projection_output, weights_in.T, preferred_element_type=jnp.float32
    )
    delta_gain_first = jnp.sum(grad_first * residual * scale_first, axis=0)
    grad_enter = (grad_middle + norm_back(grad_first * gain_first, residual, scale_first)).astype(
        jnp.bfloat16
    )
    return (
        grad_enter,
        (
            delta_gain_first,
            delta_attn_in,
            delta_attn_out,
            delta_gain_second,
            delta_router,
            delta_in,
            delta_out,
        ),
    )


def select_section(first_section, early_state, late_state):
    return jax.tree.map(
        lambda left_part, right_part: jnp.where(first_section, left_part, right_part),
        early_state,
        late_state,
    )


def shards(
    layer_input,
    cotangent,
    positions,
    routes,
    gain_one,
    attn_in,
    attn_out,
    gain_two,
    router,
    experts_in,
    experts_out,
):
    section_index = lax.axis_index("section")
    first_section = section_index == 0
    micros = layer_input.shape[0]
    tick_count = micros + 1
    weights_in, weights_out = (
        lax.all_gather(attn_in[0], "dp", axis=0, tiled=True),
        lax.all_gather(attn_out[0], "dp", axis=0, tiled=True),
    )
    params = (
        gain_one[0],
        weights_in,
        weights_out,
        gain_two[0],
        router[0],
        experts_in[0],
        experts_out[0],
    )
    nothing = jnp.zeros_like(layer_input[0])
    carried = nothing
    leaving_list = []
    saved_list = []
    for tick_index in range(tick_count):
        micro_index = jnp.clip(tick_index - section_index, 0, micros - 1)
        fresh_input = layer_input[tick_index] if tick_index < micros else nothing
        entering = jnp.where(first_section, fresh_input, carried)
        route_now = lax.dynamic_index_in_dim(routes[0], micro_index, 0, keepdims=False)
        place_now = lax.dynamic_index_in_dim(positions, micro_index, 0, keepdims=False)
        leaving, kept_state = layer_forward(entering, route_now, place_now, params)
        leaving_list.append(leaving)
        saved_list.append((entering, route_now, place_now))
        if tick_index + 1 < tick_count:
            carried = shifted(leaving, "section", 1)
    totals = None
    incoming = nothing
    grad_list = []
    for tick_index in range(tick_count):
        early_state = saved_list[max(tick_index - 1, 0)]
        late_state = saved_list[min(tick_index + 1, tick_count - 1)]
        picked = select_section(first_section, early_state, late_state)
        unused, kept_state = layer_forward(picked[0], picked[1], picked[2], params)
        fresh_grad = cotangent[tick_index] if tick_index < micros else nothing
        arriving = jnp.where(first_section, incoming, fresh_grad)
        grad_enter, deltas = layer_backward(kept_state, arriving, params)
        grad_list.append(grad_enter)
        totals = deltas if totals is None else jax.tree.map(jnp.add, totals, deltas)
        if tick_index + 1 < tick_count:
            incoming = shifted(grad_enter, "section", -1)
    hidden = jnp.stack(
        [
            jnp.where(first_section, leaving_list[micro_number], leaving_list[micro_number + 1])
            for micro_number in range(micros)
        ]
    )[None]
    input_grad = jnp.stack(
        [
            jnp.where(first_section, grad_list[micro_number + 1], grad_list[micro_number])
            for micro_number in range(micros)
        ]
    )[None]
    (
        delta_gain_first,
        delta_attn_in,
        delta_attn_out,
        delta_gain_second,
        delta_router,
        delta_in,
        delta_out,
    ) = totals
    shard_in, shard_out = (
        lax.psum_scatter(delta_attn_in, ("dp", "expert"), scatter_dimension=0, tiled=True),
        lax.psum_scatter(delta_attn_out, ("dp", "expert"), scatter_dimension=0, tiled=True),
    )
    owned_in, owned_out = (
        lax.psum_scatter(
            delta_in.astype(jnp.bfloat16), "dp", scatter_dimension=1, tiled=True
        ).astype(jnp.float32),
        lax.psum_scatter(
            delta_out.astype(jnp.bfloat16), "dp", scatter_dimension=1, tiled=True
        ).astype(jnp.float32),
    )
    sum_first, sum_second, sum_router = lax.psum(
        (delta_gain_first, delta_gain_second, delta_router), ("dp", "expert")
    )
    return (
        hidden,
        input_grad,
        sum_first[None],
        shard_in[None],
        shard_out[None],
        sum_second[None],
        sum_router[None],
        owned_in[None],
        owned_out[None],
    )


def solution(mesh):
    in_specs = (
        P(None, ("dp", "expert"), None),
        P(None, ("dp", "expert"), None),
        P(None, ("dp", "expert")),
        P("section", None, ("dp", "expert"), None),
        P("section", None),
        P("section", "dp", None),
        P("section", "dp", None),
        P("section", None),
        P("section", None, None),
        P("section", "expert", None, None),
        P("section", "expert", None, None),
    )
    out_specs = (
        P("section", None, ("dp", "expert"), None),
        P("section", None, ("dp", "expert"), None),
        P("section", None),
        P("section", ("dp", "expert"), None),
        P("section", ("dp", "expert"), None),
        P("section", None),
        P("section", None, None),
        P("section", "expert", "dp", None),
        P("section", "expert", "dp", None),
    )
    return jax.shard_map(shards, mesh=mesh, in_specs=in_specs, out_specs=out_specs, check_vma=False)
```

profile of v0, /device:TPU:0, one launch (start us, length us, event | category | flops | bytes accessed | tf_op | source)
XLA Modules:
  0.0 1600.2 jit_solution(14398626036409096882)
XLA Ops:
  16.2 76.9 %all-gather.5.cloned.1.call-done = bf16[1,1024,2048]{2,1,0:T(8,128)(2,1)} async-done(((bf16[1,256,2048]{2,1,0:T(8,128)(2,1)}), bf16[1,1024,2048]{2,1,0:T(8,128)(2,1)}) %all-gather.5.cloned.1.call-update) | async-done | bytes 4194320 | tf_op jit(solution)/shard_map/all_gather | solution.py:423
  98.7 40.5 %all-gather.7.cloned.1.call-done = bf16[1,1024,1024]{2,1,0:T(8,128)(2,1)} async-done(((bf16[1,256,1024]{2,1,0:T(8,128)(2,1)}), bf16[1,1024,1024]{2,1,0:T(8,128)(2,1)}) %all-gather.7.cloned.1.call-update) | async-done | bytes 2097168 | tf_op jit(solution)/shard_map/all_gather | solution.py:424
  143.3 29.5 %all_to_all.90 = bf16[8,128,1024]{2,0,1:T(8,128)(2,1)S(1)} all-to-all(bf16[8,128,1024]{2,0,1:T(8,128)(2,1)S(1)} %copy.727), channel_id=1, replica_groups=mesh['section'=2,'dp'=4,'expert'=4] {'expert'}, dimensions={1} | all-to-all | bytes 4194304 | tf_op jit(solution)/shard_map/all_to_all | solution.py:261
  172.9 10.4 fusion.16
  196.4 18.2 %all-to-all-done.1 = bf16[8,128,1024]{2,0,1:T(8,128)(2,1)S(1)} async-done(((bf16[8,128,1024]{2,0,1:T(8,128)(2,1)}), bf16[8,128,1024]{2,0,1:T(8,128)(2,1)S(1)}, u32[]{:S(2)}, u32[]{:S(2)}) %all-to-all-start.1) | async-done | bytes 2097184 | tf_op jit(solution)/shard_map/all_to_all | solution.py:263
  255.5 12.8 all-to-all-done.2
  268.3 10.9 fusion.14
  297.2 19.3 %all-to-all-done.3 = bf16[8,128,1024]{2,0,1:T(8,128)(2,1)} async-done(((bf16[8,128,1024]{2,0,1:T(8,128)(2,1)}), bf16[8,128,1024]{2,0,1:T(8,128)(2,1)}, u32[]{:S(2)}, u32[]{:S(2)}) %all-to-all-start.3) | async-done | bytes 2097184 | tf_op jit(solution)/shard_map/all_to_all | solution.py:263
  353.0 29.6 %all_to_all.91 = bf16[8,128,1024]{2,0,1:T(8,128)(2,1)} all-to-all(bf16[8,128,1024]{2,0,1:T(8,128)(2,1)S(1)} %copy.785), channel_id=1, replica_groups=mesh['section'=2,'dp'=4,'expert'=4] {'expert'}, dimensions={1} | all-to-all | bytes 4194304 | tf_op jit(solution)/shard_map/all_to_all | solution.py:261
  414.3 19.5 %all-to-all-done.9 = bf16[8,128,1024]{2,0,1:T(8,128)(2,1)} async-done(((bf16[8,128,1024]{2,0,1:T(8,128)(2,1)}), bf16[8,128,1024]{2,0,1:T(8,128)(2,1)}, u32[]{:S(2)}, u32[]{:S(2)}) %all-to-all-start.9) | async-done | bytes 2097184 | tf_op jit(solution)/shard_map/all_to_all | solution.py:263
  477.4 14.4 all-to-all-done.6
  491.7 9.2 multiply_convert_fusion.8
  501.0 10.1 fusion.108
  610.3 20.0 %all-to-all-done.10 = bf16[8,128,1024]{2,0,1:T(8,128)(2,1)} async-done(((bf16[8,128,1024]{2,0,1:T(8,128)(2,1)}), bf16[8,128,1024]{2,0,1:T(8,128)(2,1)}, u32[]{:S(2)}, u32[]{:S(2)}) %all-to-all-start.10) | async-done | bytes 2097184 | tf_op jit(solution)/shard_map/all_to_all | solution.py:336
  630.3 9.2 multiply_convert_fusion.5
  639.5 10.1 fusion.111
  732.3 10.8 fusion.143
  743.2 10.8 fusion.140
  758.3 17.3 %add_convert_fusion.1 = bf16[8,512,1024]{2,1,0:T(8,128)(2,1)} fusion(f32[8,512,1024]{2,1,0:T(8,128)} %fusion.143, f32[8,512,1024]{2,1,0:T(8,128)} %fusion.140, bf16[8,128,512]{2,1,0:T(8,128)(2,1)S(1)} %copy-done.22, bf16[8,128,1024]{2,0,1:T(8,128)(2,1)} %all-to-all-done.14), kind=kOutput, calls=%fused_computation.19 | convolution fusion | flops 1086324736 | bytes 45088768 | tf_op jit(solution)/shard_map/erf,erd->efd/dot_general | solution.py:192
  776.8 17.7 %fusion.168 = f32[8,1024,1024]{2,1,0:T(8,128)} fusion(bf16[8,128,1024]{1,2,0:T(8,128)(2,1)} %copy.849, bf16[8,128,512]{2,1,0:T(8,128)(2,1)} %copy-done.47, bf16[8,128,512]{2,1,0:T(8,128)(2,1)S(1)} %copy-done.46), kind=kOutput, calls=%fused_computation.189 | convolution fusion | flops 2151677952 | bytes 37748736 | tf_op jit(solution)/shard_map/erd,erf->edf/dot_general | solution.py:198
  794.6 13.4 fusion.167
  817.1 29.7 %add_convert_fusion = bf16[8,1024,1024]{2,1,0:T(8,128)(2,1)} fusion(f32[8,1024,1024]{2,1,0:T(8,128)} %fusion.168, f32[8,1024,1024]{2,1,0:T(8,128)} %fusion.167, bf16[8,128,1024]{1,2,0:T(8,128)(2,1)} %copy.851, bf16[8,128,512]{2,1,0:T(8,128)(2,1)} %get-tuple-element.49, bf16[8,128,512]{2,1,0:T(8,128)(2,1)S(1)} %get-tuple-element.48), kind=kOutput, calls=%fused_computation | convolution fusion | flops 2176843776 | bytes 88080384 | tf_op jit(solution)/shard_map/erd,erf->edf/dot_general | solution.py:198
  846.8 9.6 fusion.114
  870.7 18.2 %all-to-all-done.16 = bf16[8,128,1024]{2,0,1:T(8,128)(2,1)} async-done(((bf16[8,128,1024]{2,0,1:T(8,128)(2,1)}), bf16[8,128,1024]{2,0,1:T(8,128)(2,1)}, u32[]{:S(2)}, u32[]{:S(2)}) %all-to-all-start.16) | async-done | bytes 2097184 | tf_op jit(solution)/shard_map/all_to_all | solution.py:338
  950.0 28.0 %all_to_all.92 = bf16[8,128,1024]{2,0,1:T(8,128)(2,1)S(1)} all-to-all(bf16[8,128,1024]{2,0,1:T(8,128)(2,1)S(1)} %copy.767), channel_id=1, replica_groups=mesh['section'=2,'dp'=4,'expert'=4] {'expert'}, dimensions={1} | all-to-all | bytes 4194304 | tf_op jit(solution)/shard_map/all_to_all | solution.py:261
  978.0 10.7 fusion.12
  997.1 22.5 %all-to-all-done.5 = bf16[8,128,1024]{2,0,1:T(8,128)(2,1)S(1)} async-done(((bf16[8,128,1024]{2,0,1:T(8,128)(2,1)}), bf16[8,128,1024]{2,0,1:T(8,128)(2,1)S(1)}, u32[]{:S(2)}, u32[]{:S(2)}) %all-to-all-start.5) | async-done | bytes 2097184 | tf_op jit(solution)/shard_map/all_to_all | solution.py:263
  1030.0 43.1 %all-reduce = (f32[1,1024]{1,0:T(1,128)}, f32[1,1024]{1,0:T(1,128)}) all-reduce(f32[1,1024]{1,0:T(1,128)S(1)} %bitcast.861, f32[1,1024]{1,0:T(1,128)S(1)} %bitcast.860), channel_id=1, replica_groups=mesh['section'=2,'dp'=4,'expert'=4] {'dp','expert'}, use_global_device_ids=true, to_apply=%region_72.73 | all-reduce | flops 2048 | bytes 16384 | tf_op jit(solution)/shard_map/psum | solution.py:498
  1078.0 124.7 %reduce-scatter.9.cloned.1.call-done = bf16[8,256,1024]{2,1,0:T(8,128)(2,1)} async-done(((bf16[8,1024,1024]{2,1,0:T(8,128)(2,1)}), bf16[8,256,1024]{2,1,0:T(8,128)(2,1)}) %reduce-scatter.9.cloned.1.call-update) | async-done | bytes 4194320 | tf_op jit(solution)/shard_map/reduce_scatter | solution.py:491
  1209.4 104.7 %all-reduce.3.cloned.1.call-done = f32[1,1024,32]{1,2,0:T(8,128)} async-done(((f32[1,1024,32]{1,2,0:T(8,128)}), f32[1,1024,32]{1,2,0:T(8,128)}) %all-reduce.3.cloned.1.call-update) | async-done | bytes 131088 | tf_op jit(solution)/shard_map/psum | solution.py:498
  1314.1 97.0 %reduce-scatter.7.cloned.1.call-done = f32[64,1024]{1,0:T(8,128)} async-done(((f32[1024,1024]{1,0:T(8,128)}), f32[64,1024]{1,0:T(8,128)}) %reduce-scatter.7.cloned.1.call-update) | async-done | bytes 262160 | tf_op jit(solution)/shard_map/reduce_scatter | solution.py:488
  1411.1 180.4 %reduce-scatter.5.cloned.1.call-done = f32[64,2048]{1,0:T(8,128)} async-done(((f32[1024,2048]{1,0:T(8,128)}), f32[64,2048]{1,0:T(8,128)}) %reduce-scatter.5.cloned.1.call-update) | async-done | bytes 524304 | tf_op jit(solution)/shard_map/reduce_scatter | solution.py:487
  (827 shorter events, 503.2 us)
Async XLA Ops:
  7.2 188.8 %copy-start = (bf16[1,1024,32]{1,2,0:T(8,128)(2,1)S(1)}, bf16[1,1024,32]{1,2,0:T(8,128)(2,1)}, u32[]{:S(2)}) copy-start(bf16[1,1024,32]{1,2,0:T(8,128)(2,1)} %param.19) | copy-start | bytes 196612
  7.2 85.9 %all-gather.5.cloned.1.call-start = ((), (), s32[]{:S(2)}) async-start(), calls=%async_computation.27 | async-start | bytes 5242880 | tf_op jit(solution)/shard_map/all_gather | solution.py:423
  7.9 131.2 %all-gather.7.cloned.1.call-start = ((), (), s32[]{:S(2)}) async-start(), calls=%async_computation.28 | async-start | bytes 2621440 | tf_op jit(solution)/shard_map/all_gather | solution.py:424
  8.7 84.4 %copy-start.78 = (f32[1,1024]{1,0:T(1,128)S(1)}, f32[1,1024]{1,0:T(1,128)}, u32[]{:S(2)}) copy-start(f32[1,1024]{1,0:T(1,128)} %param.15) | copy-start | bytes 12292
  9.5 86.7 %copy-start.136 = (s32[1,1,64,8]{2,3,1,0:T(8,128)}, s32[1,1,64,8]{2,3,1,0:T(8,128)S(1)}, u32[]{:S(2)}) copy-start(s32[1,1,64,8]{2,3,1,0:T(8,128)S(1)} %get-tuple-element.109) | copy-start | bytes 6148
  9.5 86.7 %copy-start.138 = (s32[1,1,64,8]{2,3,1,0:T(8,128)}, s32[1,1,64,8]{2,3,1,0:T(8,128)S(1)}, u32[]{:S(2)}) copy-start(s32[1,1,64,8]{2,3,1,0:T(8,128)S(1)} %get-tuple-element.111) | copy-start | bytes 6148
  15.4 332.2 %copy-start.118 = (pred[64,64]{0,1:T(8,128)(4,1)}, pred[64,64]{0,1:T(8,128)(4,1)S(1)}, u32[]{:S(2)}) copy-start(pred[64,64]{0,1:T(8,128)(4,1)S(1)} %iota_compare_fusion.91) | copy-start | bytes 12292
  187.4 27.2 %all-to-all-start.1 = ((bf16[8,128,1024]{2,0,1:T(8,128)(2,1)}), bf16[8,128,1024]{2,0,1:T(8,128)(2,1)S(1)}, u32[]{:S(2)}, u32[]{:S(2)}) async-start(bf16[8,128,1024]{2,0,1:T(8,128)(2,1)} %copy.729), calls=%async_computation.1 | async-start | bytes 4194304 | tf_op jit(solution)/shard_map/all_to_all | solution.py:263
  220.3 2.3 collective-permute-start
  223.4 353.4 %copy-start.23 = (bf16[64,1024]{1,0:T(8,128)(2,1)}, bf16[64,1024]{1,0:T(8,128)(2,1)S(1)}, u32[]{:S(2)}) copy-start(bf16[64,1024]{1,0:T(8,128)(2,1)S(1)} %get-tuple-element.42) | copy-start | bytes 393220
  237.8 30.6 %all-to-all-start.2 = ((bf16[8,128,1024]{2,0,1:T(8,128)(2,1)}), bf16[8,128,1024]{2,0,1:T(8,128)(2,1)}, u32[]{:S(2)}, u32[]{:S(2)}) async-start(bf16[8,128,1024]{2,0,1:T(8,128)(2,1)} %copy.747), calls=%async_computation.2 | async-start | bytes 4194304 | tf_op jit(solution)/shard_map/all_to_all | solution.py:261
  286.7 29.8 %all-to-all-start.3 = ((bf16[8,128,1024]{2,0,1:T(8,128)(2,1)}), bf16[8,128,1024]{2,0,1:T(8,128)(2,1)}, u32[]{:S(2)}, u32[]{:S(2)}) async-start(bf16[8,128,1024]{2,0,1:T(8,128)(2,1)} %copy.749), calls=%async_computation.3 | async-start | bytes 4194304 | tf_op jit(solution)/shard_map/all_to_all | solution.py:263
  326.2 2.3 collective-permute-start.1
  404.9 29.0 %all-to-all-start.9 = ((bf16[8,128,1024]{2,0,1:T(8,128)(2,1)}), bf16[8,128,1024]{2,0,1:T(8,128)(2,1)}, u32[]{:S(2)}, u32[]{:S(2)}) async-start(bf16[8,128,1024]{2,0,1:T(8,128)(2,1)} %copy.789), calls=%async_computation.9 | async-start | bytes 4194304 | tf_op jit(solution)/shard_map/all_to_all | solution.py:263
  433.8 28.9 %all-to-all-start.11 = ((bf16[8,128,1024]{2,0,1:T(8,128)(2,1)}), bf16[8,128,1024]{2,0,1:T(8,128)(2,1)}, u32[]{:S(2)}, u32[]{:S(2)}) async-start(bf16[8,128,1024]{2,0,1:T(8,128)(2,1)} %copy.811), calls=%async_computation.11 | async-start | bytes 4194304 | tf_op jit(solution)/shard_map/all_to_all | solution.py:261
  462.7 29.1 %all-to-all-start.6 = ((bf16[8,128,1024]{2,0,1:T(8,128)(2,1)}), bf16[8,128,1024]{2,0,1:T(8,128)(2,1)}, u32[]{:S(2)}, u32[]{:S(2)}) async-start(bf16[8,128,1024]{2,0,1:T(8,128)(2,1)} %copy.781), calls=%async_computation.6 | async-start | bytes 4194304 | tf_op jit(solution)/shard_map/all_to_all | solution.py:336
  513.6 29.3 %all-to-all-start.8 = ((bf16[8,128,1024]{2,0,1:T(8,128)(2,1)}), bf16[8,128,1024]{2,0,1:T(8,128)(2,1)}, u32[]{:S(2)}, u32[]{:S(2)}) async-start(bf16[8,128,1024]{2,0,1:T(8,128)(2,1)} %copy.787), calls=%async_computation.8 | async-start | bytes 4194304 | tf_op jit(solution)/shard_map/all_to_all | solution.py:338
  542.9 29.4 %all-to-all-start.13 = ((bf16[8,128,1024]{2,0,1:T(8,128)(2,1)}), bf16[8,128,1024]{2,0,1:T(8,128)(2,1)}, u32[]{:S(2)}, u32[]{:S(2)}) async-start(bf16[8,128,1024]{2,0,1:T(8,128)(2,1)} %copy.815), calls=%async_computation.13 | async-start | bytes 4194304 | tf_op jit(solution)/shard_map/all_to_all | solution.py:263
  572.3 28.9 %all-to-all-start.15 = ((bf16[8,128,1024]{2,0,1:T(8,128)(2,1)}), bf16[8,128,1024]{2,0,1:T(8,128)(2,1)}, u32[]{:S(2)}, u32[]{:S(2)}) async-start(bf16[8,128,1024]{2,0,1:T(8,128)(2,1)} %copy.837), calls=%async_computation.15 | async-start | bytes 4194304 | tf_op jit(solution)/shard_map/all_to_all | solution.py:261
  578.6 5.7 collective-permute-start.2
  601.2 29.1 %all-to-all-start.10 = ((bf16[8,128,1024]{2,0,1:T(8,128)(2,1)}), bf16[8,128,1024]{2,0,1:T(8,128)(2,1)}, u32[]{:S(2)}, u32[]{:S(2)}) async-start(bf16[8,128,1024]{2,0,1:T(8,128)(2,1)} %copy.807), calls=%async_computation.10 | async-start | bytes 4194304 | tf_op jit(solution)/shard_map/all_to_all | solution.py:336
  652.2 29.3 %all-to-all-start.12 = ((bf16[8,128,1024]{2,0,1:T(8,128)(2,1)}), bf16[8,128,1024]{2,0,1:T(8,128)(2,1)}, u32[]{:S(2)}, u32[]{:S(2)}) async-start(bf16[8,128,1024]{2,0,1:T(8,128)(2,1)} %copy.813), calls=%async_computation.12 | async-start | bytes 4194304 | tf_op jit(solution)/shard_map/all_to_all | solution.py:338
  681.5 31.1 %all-to-all-start.17 = ((bf16[8,128,1024]{2,0,1:T(8,128)(2,1)}), bf16[8,128,1024]{2,0,1:T(8,128)(2,1)}, u32[]{:S(2)}, u32[]{:S(2)}) async-start(bf16[8,128,1024]{2,0,1:T(8,128)(2,1)} %copy.841), calls=%async_computation.17 | async-start | bytes 4194304 | tf_op jit(solution)/shard_map/all_to_all | solution.py:263
  711.2 5.5 collective-permute-start.3
  727.4 30.9 %all-to-all-start.14 = ((bf16[8,128,1024]{2,0,1:T(8,128)(2,1)}), bf16[8,128,1024]{2,0,1:T(8,128)(2,1)}, u32[]{:S(2)}, u32[]{:S(2)}) async-start(bf16[8,128,1024]{2,0,1:T(8,128)(2,1)} %copy.833), calls=%async_computation.14 | async-start | bytes 4194304 | tf_op jit(solution)/shard_map/all_to_all | solution.py:336
  732.2 341.7 %reduce-scatter.11.cloned.1.call-start = ((), (), s32[]{:S(2)}) async-start(), calls=%async_computation.26 | async-start | bytes 10485760 | tf_op jit(solution)/shard_map/reduce_scatter | solution.py:494
  775.6 427.1 %reduce-scatter.9.cloned.1.call-start = ((), (), s32[]{:S(2)}) async-start(), calls=%async_computation.25 | async-start | bytes 20971520 | tf_op jit(solution)/shard_map/reduce_scatter | solution.py:491
  858.9 30.1 %all-to-all-start.16 = ((bf16[8,128,1024]{2,0,1:T(8,128)(2,1)}), bf16[8,128,1024]{2,0,1:T(8,128)(2,1)}, u32[]{:S(2)}, u32[]{:S(2)}) async-start(bf16[8,128,1024]{2,0,1:T(8,128)(2,1)} %copy.839), calls=%async_computation.16 | async-start | bytes 4194304 | tf_op jit(solution)/shard_map/all_to_all | solution.py:338
  863.6 450.5 %all-reduce.3.cloned.1.call-start = ((), (), s32[]{:S(2)}) async-start(), calls=%async_computation.24 | async-start | bytes 262144 | tf_op jit(solution)/shard_map/psum | solution.py:498
  870.7 540.4 %reduce-scatter.7.cloned.1.call-start = ((), (), s32[]{:S(2)}) async-start(), calls=%async_computation.23 | async-start | bytes 4456448 | tf_op jit(solution)/shard_map/reduce_scatter | solution.py:488
  898.1 693.5 %reduce-scatter.5.cloned.1.call-start = ((), (), s32[]{:S(2)}) async-start(), calls=%async_computation.22 | async-start | bytes 8912896 | tf_op jit(solution)/shard_map/reduce_scatter | solution.py:487
  992.8 26.7 %all-to-all-start.5 = ((bf16[8,128,1024]{2,0,1:T(8,128)(2,1)}), bf16[8,128,1024]{2,0,1:T(8,128)(2,1)S(1)}, u32[]{:S(2)}, u32[]{:S(2)}) async-start(bf16[8,128,1024]{2,0,1:T(8,128)(2,1)} %copy.769), calls=%async_computation.5 | async-start | bytes 4194304 | tf_op jit(solution)/shard_map/all_to_all | solution.py:263
  (194 other events, 1281.9 us)
Sparse Core Ops, SparseCore 0:
  9.6 83.4 all-gather.4
  94.7 44.4 all-gather.6
  775.7 142.5 reduce-scatter.10
  920.5 282.1 reduce-scatter.8
  1208.9 105.1 all-reduce.2
  1316.9 94.1 reduce-scatter.6
  1414.1 177.4 reduce-scatter.4
where the time goes:
time: 1610 us; the launch traced here: 1600 us
  waiting for transfers between devices  799 us (50%)
  matrix products  364 us (23%)
  local copies, waits for them, and re-layouts  150 us (9%)
  blocking collectives  130 us (8%)
  starting transfers between devices  74.8 us (5%)
  other arithmetic  64.4 us (4%)
  between operations  17.7 us (1%)
    reduce_scatter x1, waiting for transfers between devices, shards(): lax.psum_scatter(delta_attn_in, ('dp', 'expert'), scatter_dimension=0, ti...  180 us
    reduce_scatter x1, waiting for transfers between devices, shards(): lax.psum_scatter(delta_in.astype(jnp.bfloat16), 'dp', scatter_dimension=1...  125 us
    psum x1, waiting for transfers between devices, shards(): lax.psum((delta_gain_first, delta_gain_second, delta_router), ('dp', 'exp...  105 us
    reduce_scatter x1, waiting for transfers between devices, shards(): lax.psum_scatter(delta_attn_out, ('dp', 'expert'), scatter_dimension=0, t...  97 us
    all_to_all x3, blocking collectives, layer_forward(): lax.all_to_all(outgoing, 'expert', split_axis=1, concat_axis=1, tiled=True)  87.1 us
    all_to_all x6, waiting for transfers between devices, layer_forward(): lax.all_to_all(produced, 'expert', split_axis=1, concat_axis=1, tiled=True)  79.5 us
    all_gather x1, waiting for transfers between devices, shards(): lax.all_gather(attn_in[0], 'dp', axis=0, tiled=True)  76.9 us
    dot_general x3, matrix products, expert_backward(): jnp.einsum('erd,erf->edf', arrived, grad_pair, preferred_element_type=jnp...  60.8 us
  transfers between devices with their start and end apart: 26, of which 21 were waited for; matrix products, arithmetic and copies ran while one was open for 24% of the time, Pallas kernels for 0%

commit v1 on v0

v1 whole, which is shorter than its diff:
```python
import functools

import jax
import jax.numpy as jnp
from jax import lax
from jax.experimental import pallas as pl
from jax.experimental.pallas import tpu as pltpu
from jax.sharding import PartitionSpec as P

MODEL_WIDTH = 1024
QUERY_HEADS = 16
KEY_VALUE_HEADS = 8
HEAD_SIZE = 64
FF = 512
EXPERTS = 32
TOPK = 8

QUERY_WIDTH = QUERY_HEADS * HEAD_SIZE
KEY_WIDTH = KEY_VALUE_HEADS * HEAD_SIZE
PROJECTED = QUERY_WIDTH + 2 * KEY_WIDTH
LANES = 128
HALF = HEAD_SIZE // 2

epsilon = 1e-06
rotary_base = 10000.0

F32 = jnp.float32
BF16 = jnp.bfloat16
MESH = pl.DeviceIdType.MESH
VMEM_LIMIT = 60 * 1024 * 1024


def dot_nn(a, b):
    return lax.dot_general(a, b, (((1,), (0,)), ((), ())), preferred_element_type=F32)


def dot_nt(a, b):
    return lax.dot_general(a, b, (((1,), (1,)), ((), ())), preferred_element_type=F32)


def dot_tn(a, b):
    return lax.dot_general(a, b, (((0,), (0,)), ((), ())), preferred_element_type=F32)


def row_scale(values):
    return lax.rsqrt(jnp.mean(values * values, axis=-1, keepdims=True) + epsilon)


def norm_back(grad_normed, inputs, scale):
    return scale * grad_normed - inputs * (scale * scale * scale) * jnp.mean(
        grad_normed * inputs, axis=-1, keepdims=True
    )


def lane_of(shape):
    return lax.broadcasted_iota(jnp.int32, shape, 1)


def turned(tile, low):
    return jnp.where(low, pltpu.roll(tile, LANES - HALF, 1), pltpu.roll(tile, HALF, 1))


def vmem_spec():
    return pl.BlockSpec(memory_space=pltpu.VMEM)


def any_spec():
    return pl.BlockSpec(memory_space=pl.ANY)


def gather_kernel(planes, owners, rows, in_ref, out_ref, win_ref, wout_ref, local_sem, z_send, z_recv, p_send, p_recv, c_send, c_recv):
    section = lax.axis_index("section")
    plane = lax.axis_index("dp")
    own = lax.axis_index("expert")
    part = rows // owners
    barrier = pltpu.get_barrier_semaphore()
    for step in range(1, planes):
        pl.semaphore_signal(barrier, inc=1, device_id={"dp": (plane + step) % planes}, device_id_type=MESH)
    for step in range(1, owners):
        pl.semaphore_signal(barrier, inc=1, device_id={"expert": (own + step) % owners}, device_id_type=MESH)
    pl.semaphore_signal(barrier, inc=1, device_id={"section": 1 - section}, device_id_type=MESH)
    pl.semaphore_wait(barrier, planes + owners - 1)

    pairs = ((in_ref, win_ref), (out_ref, wout_ref))
    locals_ = []
    for which, (source, full) in enumerate(pairs):
        copy = pltpu.make_async_copy(
            source.at[0], full.at[section, pl.ds(plane * rows, rows)], local_sem.at[which]
        )
        copy.start()
        locals_.append(copy)
    z_copies = {}
    for which, (source, full) in enumerate(pairs):
        for step in range(1, planes):
            copy = pltpu.make_async_remote_copy(
                src_ref=source.at[0, pl.ds(own * part, part)],
                dst_ref=full.at[section, pl.ds(plane * rows + own * part, part)],
                send_sem=z_send.at[step, which],
                recv_sem=z_recv.at[step, which],
                device_id={"dp": (plane + step) % planes},
                device_id_type=MESH,
            )
            copy.start()
            z_copies[which, step] = copy
    core_copies = []

    def push(which, slab, number):
        full = pairs[which][1]
        here = full.at[section, pl.ds(slab * rows, rows)]
        copy = pltpu.make_async_remote_copy(
            src_ref=here,
            dst_ref=here,
            send_sem=c_send.at[number, which],
            recv_sem=c_recv.at[number, which],
            device_id={"section": 1 - section},
            device_id_type=MESH,
        )
        copy.start()
        core_copies.append(copy)

    p_copies = {}
    for which, (source, full) in enumerate(pairs):
        locals_[which].wait()
        push(which, plane, 0)
        for step in range(1, planes):
            z_copies[which, step].wait_recv()
            origin = (plane + planes - step) % planes
            here = full.at[section, pl.ds(origin * rows + own * part, part)]
            for turn in range(1, owners):
                copy = pltpu.make_async_remote_copy(
                    src_ref=here,
                    dst_ref=here,
                    send_sem=p_send.at[step, turn, which],
                    recv_sem=p_recv.at[step, turn, which],
                    device_id={"expert": (own + turn) % owners},
                    device_id_type=MESH,
                )
                copy.start()
                p_copies[which, step, turn] = copy
    for which in range(2):
        for step in range(1, planes):
            for turn in range(1, owners):
                p_copies[which, step, turn].wait_recv()
            push(which, (plane + planes - step) % planes, step)
    for copy in z_copies.values():
        copy.wait_send()
    for copy in p_copies.values():
        copy.wait_send()
    for copy in core_copies:
        copy.wait()


def gather_weights(attn_in, attn_out):
    planes = lax.axis_size("dp")
    owners = lax.axis_size("expert")
    rows = attn_in.shape[1]
    sems = pltpu.SemaphoreType.DMA
    return pl.pallas_call(
        functools.partial(gather_kernel, planes, owners, rows),
        out_shape=(
            jax.ShapeDtypeStruct((2, planes * rows, attn_in.shape[2]), BF16),
            jax.ShapeDtypeStruct((2, planes * rows, attn_out.shape[2]), BF16),
        ),
        in_specs=[any_spec(), any_spec()],
        out_specs=(any_spec(), any_spec()),
        scratch_shapes=[
            sems((2,)),
            sems((planes, 2)),
            sems((planes, 2)),
            sems((planes, owners, 2)),
            sems((planes, owners, 2)),
            sems((planes, 2)),
            sems((planes, 2)),
        ],
        compiler_params=pltpu.CompilerParams(collective_id=0, has_side_effects=True, vmem_limit_bytes=VMEM_LIMIT),
        name="gather_weights",
    )(attn_in, attn_out)


def attention_forward_kernel(
    layer, x_ref, gain_one_ref, win_all, wout_all, gain_two_ref, router_ref, hot_ref, cos_ref, sin_ref,
    middle_ref, normed_ref, gate_ref, query_ref, key_ref, value_ref, attended_ref, log_ref,
    projected_ref, win_ref, wout_ref, sem,
):
    win_copy = pltpu.make_async_copy(win_all.at[layer], win_ref, sem.at[0])
    wout_copy = pltpu.make_async_copy(wout_all.at[layer], wout_ref, sem.at[1])
    win_copy.start()
    wout_copy.start()
    tokens = x_ref.shape[0]
    lane = lane_of((tokens, LANES))
    low = lane % HEAD_SIZE < HALF
    left = lane < HEAD_SIZE
    cosine, sine = cos_ref[...], sin_ref[...]
    residual = x_ref[...].astype(F32)
    normed_one = (residual * row_scale(residual) * gain_one_ref[...]).astype(BF16)
    win_copy.wait()
    projected_ref[...] = dot_nn(normed_one, win_ref[...])
    for tile in range(QUERY_WIDTH // LANES):
        columns = slice(tile * LANES, (tile + 1) * LANES)
        part = projected_ref[:, columns]
        query_ref[:, columns] = (part * cosine + turned(part, low) * sine).astype(BF16)
    for tile in range(KEY_WIDTH // LANES):
        first = slice(2 * tile * LANES, (2 * tile + 1) * LANES)
        second = slice((2 * tile + 1) * LANES, (2 * tile + 2) * LANES)
        part = projected_ref[:, QUERY_WIDTH + tile * LANES : QUERY_WIDTH + (tile + 1) * LANES]
        part = part * cosine + turned(part, low) * sine
        other = pltpu.roll(part, HEAD_SIZE, 1)
        key_ref[:, first] = jnp.where(left, part, other).astype(BF16)
        key_ref[:, second] = jnp.where(left, other, part).astype(BF16)
        start = QUERY_WIDTH + KEY_WIDTH + tile * LANES
        part = projected_ref[:, start : start + LANES]
        other = pltpu.roll(part, HEAD_SIZE, 1)
        value_ref[:, first] = jnp.where(left, part, other).astype(BF16)
        value_ref[:, second] = jnp.where(left, other, part).astype(BF16)
    pair_lane = lane_of((2 * tokens, LANES))
    row = lax.broadcasted_iota(jnp.int32, (2 * tokens, tokens), 0) % tokens
    allowed = row >= lax.broadcasted_iota(jnp.int32, (2 * tokens, tokens), 1)
    logs = jnp.zeros((2 * tokens, LANES), F32)
    for head in range(KEY_VALUE_HEADS):
        columns = slice(head * LANES, (head + 1) * LANES)
        query = query_ref[:, columns]
        nothing = jnp.zeros_like(query)
        stacked = jnp.concatenate([jnp.where(left, query, nothing), jnp.where(left, nothing, query)], axis=0)
        scores = dot_nt(stacked, key_ref[:, columns]) * HEAD_SIZE ** (-0.5)
        scores = jnp.where(allowed, scores, -1e30)
        top = jnp.max(scores, axis=-1, keepdims=True)
        log_total = top + jnp.log(jnp.sum(jnp.exp(scores - top), axis=-1, keepdims=True))
        logs = jnp.where(pair_lane == head, log_total, logs)
        weights = jnp.exp(scores - log_total).astype(BF16)
        mixed = dot_nn(weights, value_ref[:, columns])
        attended_ref[:, columns] = jnp.where(left, mixed[:tokens], mixed[tokens:]).astype(BF16)
    log_ref[...] = logs
    wout_copy.wait()
    middle = residual + dot_nn(attended_ref[...], wout_ref[...])
    middle_ref[...] = middle
    normed_two = (middle * row_scale(middle) * gain_two_ref[...]).astype(BF16)
    normed_ref[...] = normed_two
    logits = dot_nn(normed_two, router_ref[...])
    chosen = hot_ref[...] > 0.0
    top = jnp.max(jnp.where(chosen, logits, -1e30), axis=-1, keepdims=True)
    grown = jnp.where(chosen, jnp.exp(jnp.where(chosen, logits - top, 0.0)), 0.0)
    gate_ref[...] = grown / jnp.sum(grown, axis=-1, keepdims=True)


def weight_scratch():
    return [
        pltpu.VMEM((MODEL_WIDTH, PROJECTED), BF16),
        pltpu.VMEM((QUERY_WIDTH, MODEL_WIDTH), BF16),
        pltpu.SemaphoreType.DMA((2,)),
    ]


def attention_forward(layer, x, gain_one, win, wout, gain_two, router, hot, cosine, sine):
    tokens = x.shape[0]
    shape = jax.ShapeDtypeStruct
    return pl.pallas_call(
        functools.partial(attention_forward_kernel, layer),
        out_shape=(
            shape((tokens, MODEL_WIDTH), F32),
            shape((tokens, MODEL_WIDTH), BF16),
            shape((tokens, LANES), F32),
            shape((tokens, QUERY_WIDTH), BF16),
            shape((tokens, 2 * KEY_WIDTH), BF16),
            shape((tokens, 2 * KEY_WIDTH), BF16),
            shape((tokens, QUERY_WIDTH), BF16),
            shape((2 * tokens, LANES), F32),
        ),
        in_specs=[vmem_spec(), vmem_spec(), any_spec(), any_spec()] + [vmem_spec()] * 5,
        out_specs=tuple(vmem_spec() for _ in range(8)),
        scratch_shapes=[pltpu.VMEM((tokens, PROJECTED), F32)] + weight_scratch(),
        compiler_params=pltpu.CompilerParams(vmem_limit_bytes=VMEM_LIMIT),
        name="attention_forward",
    )(x, gain_one[layer], win, wout, gain_two[layer], router[layer], hot[layer], cosine, sine)


def attention_backward_kernel(
    layer, x_ref, gain_one_ref, win_all, wout_all, gain_two_ref, router_ref, cos_ref, sin_ref,
    middle_ref, gate_ref, query_ref, key_ref, value_ref, attended_ref, log_ref,
    up_ref, back_ref, gate_grad_ref,
    input_grad_ref, grad_projected_ref, low_ref, normed_ref, grad_logits_ref, gain_grad_ref,
    win_ref, wout_ref, sem,
):
    win_copy = pltpu.make_async_copy(win_all.at[layer], win_ref, sem.at[0])
    wout_copy = pltpu.make_async_copy(wout_all.at[layer], wout_ref, sem.at[1])
    wout_copy.start()
    win_copy.start()
    tokens = x_ref.shape[0]
    lane = lane_of((tokens, LANES))
    low_half = lane % HEAD_SIZE < HALF
    left = lane < HEAD_SIZE
    cosine, sine = cos_ref[...], sin_ref[...]
    gates, gate_grads = gate_ref[...], gate_grad_ref[...]
    grad_picked = gates * (gate_grads - jnp.sum(gates * gate_grads, axis=-1, keepdims=True))
    grad_logits = grad_picked.astype(BF16)
    grad_logits_ref[...] = grad_logits
    grad_second = back_ref[...] + dot_nt(grad_logits, router_ref[...])
    middle = middle_ref[...]
    scale_two = row_scale(middle)
    gain_two_grad = jnp.sum(grad_second * middle * scale_two, axis=0, keepdims=True)
    upstream = up_ref[...].astype(F32)
    grad_middle = upstream + norm_back(grad_second * gain_two_ref[...], middle, scale_two)
    low = grad_middle.astype(BF16)
    low_ref[...] = low
    wout_copy.wait()
    grad_attended = dot_nt(low, wout_ref[...]).astype(BF16)
    row = lax.broadcasted_iota(jnp.int32, (2 * tokens, tokens), 0) % tokens
    allowed = row >= lax.broadcasted_iota(jnp.int32, (2 * tokens, tokens), 1)
    root = HEAD_SIZE ** (-0.5)
    pair_lane = lane_of((2 * tokens, LANES))
    logs = log_ref[...]

    def stack(tile):
        nothing = jnp.zeros_like(tile)
        return jnp.concatenate([jnp.where(left, tile, nothing), jnp.where(left, nothing, tile)], axis=0)

    def fold(wide):
        return wide + pltpu.roll(wide, HEAD_SIZE, 1)

    key_grads, value_grads = [], []
    for head in range(KEY_VALUE_HEADS):
        columns = slice(head * LANES, (head + 1) * LANES)
        query = stack(query_ref[:, columns])
        key, value = key_ref[:, columns], value_ref[:, columns]
        scores = dot_nt(query, key) * root
        log_total = jnp.sum(jnp.where(pair_lane == head, logs, 0.0), axis=-1, keepdims=True)
        probabilities = jnp.where(allowed, jnp.exp(jnp.where(allowed, scores - log_total, 0.0)), 0.0)
        grad_tile = stack(grad_attended[:, columns])
        delta = jnp.sum(
            grad_tile.astype(F32) * stack(attended_ref[:, columns]).astype(F32), axis=-1, keepdims=True
        )
        grad_scores = (probabilities * (dot_nt(grad_tile, value) - delta)).astype(BF16)
        wide = dot_nn(grad_scores, key) * root
        grad_query = jnp.where(left, wide[:tokens], wide[tokens:])
        grad_query = grad_query * cosine - turned(grad_query, low_half) * sine
        grad_projected_ref[:, columns] = grad_query.astype(BF16)
        key_grads.append(fold(dot_tn(grad_scores, query)) * root)
        value_grads.append(fold(dot_tn(probabilities.astype(BF16), grad_tile)))
    for tile in range(KEY_WIDTH // LANES):
        part = jnp.where(left, key_grads[2 * tile], key_grads[2 * tile + 1])
        part = part * cosine - turned(part, low_half) * sine
        start = QUERY_WIDTH + tile * LANES
        grad_projected_ref[:, start : start + LANES] = part.astype(BF16)
        start += KEY_WIDTH
        grad_projected_ref[:, start : start + LANES] = jnp.where(
            left, value_grads[2 * tile], value_grads[2 * tile + 1]
        ).astype(BF16)
    win_copy.wait()
    grad_first = dot_nt(grad_projected_ref[...], win_ref[...])
    residual = x_ref[...].astype(F32)
    scale_one = row_scale(residual)
    normed_ref[...] = (residual * scale_one * gain_one_ref[...]).astype(BF16)
    gain_one_grad = jnp.sum(grad_first * residual * scale_one, axis=0, keepdims=True)
    gain_grad_ref[...] = jnp.concatenate(
        [gain_one_grad, gain_two_grad, jnp.zeros((6, MODEL_WIDTH), F32)], axis=0
    )
    input_grad_ref[...] = (
        grad_middle + norm_back(grad_first * gain_one_ref[...], residual, scale_one)
    ).astype(BF16)


def attention_backward(layer, x, gain_one, win, wout, gain_two, router, cosine, sine, kept, up, back, gate_grads):
    middle, gates, query, key, value, attended, logs = kept
    tokens = x.shape[0]
    shape = jax.ShapeDtypeStruct
    return pl.pallas_call(
        functools.partial(attention_backward_kernel, layer),
        out_shape=(
            shape((tokens, MODEL_WIDTH), BF16),
            shape((tokens, PROJECTED), BF16),
            shape((tokens, MODEL_WIDTH), BF16),
            shape((tokens, MODEL_WIDTH), BF16),
            shape((tokens, LANES), BF16),
            shape((8, MODEL_WIDTH), F32),
        ),
        in_specs=[vmem_spec(), vmem_spec(), any_spec(), any_spec()] + [vmem_spec()] * 14,
        out_specs=tuple(vmem_spec() for _ in range(6)),
        scratch_shapes=weight_scratch(),
        compiler_params=pltpu.CompilerParams(vmem_limit_bytes=VMEM_LIMIT),
        name="attention_backward",
    )(x, gain_one[layer], win, wout, gain_two[layer], router[layer], cosine, sine, middle, gates, query, key, value, attended, logs,
      up, back, gate_grads)


def expert_kernel(mode, layer, owners, tokens, local, *refs):
    forward, backward = "f" in mode, "b" in mode
    refs = list(refs)
    take = refs.pop
    win_own, win_other, wout_own, wout_other = (take(0) for _ in range(4))
    middle_in = take(0) if forward else None
    gate_in = take(0)
    normed_in = take(0)
    up_in = take(0) if backward else None
    hidden_out = take(0) if forward else None
    if forward:
        plane_out, plane_gate_out = take(0), take(0)
    if backward:
        back_out, gate_grad_out = take(0), take(0)
    win, wout, win_sem, wout_sem = (take(0) for _ in range(4))
    if forward:
        normed, gates = take(0), take(0)
        x_send, x_recv, g_send, g_recv = (take(0) for _ in range(4))
        total, leaving, coming, y_send, y_recv = (take(0) for _ in range(5))
    else:
        normed, gates = normed_in, gate_in
    if backward:
        ups, u_send, u_recv = (take(0) for _ in range(3))
        back_total, back_leaving, back_coming, b_send, b_recv = (take(0) for _ in range(5))
        grads, grads_leaving, grads_coming, d_send, d_recv = (take(0) for _ in range(5))

    section = lax.axis_index("section")
    own = lax.axis_index("expert")
    rows = owners * tokens

    @pl.when(section == layer)
    def _():
        for expert in range(local):
            pltpu.make_async_copy(win_own.at[0, expert], win.at[expert], win_sem.at[expert]).start()
            pltpu.make_async_copy(wout_own.at[0, expert], wout.at[expert], wout_sem.at[expert]).start()

    @pl.when(section != layer)
    def _():
        for expert in range(local):
            pltpu.make_async_copy(win_other.at[0, expert], win.at[expert], win_sem.at[expert]).start()
            pltpu.make_async_copy(wout_other.at[0, expert], wout.at[expert], wout_sem.at[expert]).start()

    barrier = pltpu.get_barrier_semaphore()
    for step in range(1, owners):
        pl.semaphore_signal(barrier, inc=1, device_id={"expert": (own + step) % owners}, device_id_type=MESH)
    here = pl.ds(own * tokens, tokens)
    if forward:
        normed[here] = normed_in[...]
        gates[here] = gate_in[...]
    if backward:
        ups[here] = up_in[...]
    pl.semaphore_wait(barrier, owners - 1)
    moves = []

    def spread(source, buffer, send, recv):
        for step in range(1, owners):
            copy = pltpu.make_async_remote_copy(
                src_ref=source,
                dst_ref=buffer.at[here],
                send_sem=send.at[step],
                recv_sem=recv.at[step],
                device_id={"expert": (own + step) % owners},
                device_id_type=MESH,
            )
            copy.start()
            moves.append(copy)

    if forward:
        spread(normed_in, normed, x_send, x_recv)
        spread(gate_in, gates, g_send, g_recv)
    if backward:
        spread(up_in, ups, u_send, u_recv)
    for copy in moves:
        copy.wait()

    chunk = min(rows, 256)
    if backward:
        grads[...] = jnp.zeros_like(grads)

    def one_expert(expert, carry):
        pltpu.make_async_copy(win_own.at[0, 0], win.at[expert], win_sem.at[expert]).wait()
        pltpu.make_async_copy(wout_own.at[0, 0], wout.at[expert], wout_sem.at[expert]).wait()
        mine = own * local + expert

        def one_chunk(number, carry):
            span = pl.ds(number * chunk, chunk)
            x = normed[span]
            lane = lane_of((chunk, LANES))
            gate = jnp.sum(jnp.where(lane == mine, gates[span], 0.0), axis=-1, keepdims=True)
            pair = dot_nn(x, win[expert])
            gate_part, up_part = pair[:, :FF], pair[:, FF:]
            sigmoid = 1.0 / (1.0 + jnp.exp(-gate_part))
            silu = gate_part * sigmoid
            activated = silu * up_part
            if forward:
                term = dot_nn((activated * gate).astype(BF16), wout[expert])

                @pl.when(expert == 0)
                def _():
                    total[span] = term

                @pl.when(expert > 0)
                def _():
                    total[span] += term

            if backward:
                inner = dot_nt(ups[span], wout[expert])
                gate_grad = jnp.sum(activated * inner, axis=-1, keepdims=True)
                grads[span] = jnp.where(lane == mine, gate_grad, grads[span])
                grad_activated = inner * gate
                grad_gate = grad_activated * up_part * sigmoid * (1.0 + gate_part * (1.0 - sigmoid))
                grad_up = grad_activated * silu
                grad_pair = jnp.concatenate([grad_gate.astype(BF16), grad_up.astype(BF16)], axis=-1)
                term_back = dot_nt(grad_pair, win[expert])

                @pl.when(expert == 0)
                def _():
                    back_total[span] = term_back

                @pl.when(expert > 0)
                def _():
                    back_total[span] += term_back

            return carry

        return lax.fori_loop(0, rows // chunk, one_chunk, carry)

    lax.fori_loop(0, local, one_expert, 0)

    def send_back(source, out, arriving, send, recv):
        copies = []
        for step in range(1, owners):
            target = (own + step) % owners
            out[step] = source[pl.ds(target * tokens, tokens)].astype(out.dtype)
            copy = pltpu.make_async_remote_copy(
                src_ref=out.at[step],
                dst_ref=arriving.at[step],
                send_sem=send.at[step],
                recv_sem=recv.at[step],
                device_id={"expert": target},
                device_id_type=MESH,
            )
            copy.start()
            copies.append(copy)
        return copies

    if backward:
        back_copies = send_back(back_total, back_leaving, back_coming, b_send, b_recv)
        grad_copies = send_back(grads, grads_leaving, grads_coming, d_send, d_recv)
    if forward:
        mix_copies = send_back(total, leaving, coming, y_send, y_recv)
        plane_out[...] = normed[...]
        plane_gate_out[...] = gates[...]

    def finish(source, arriving, copies):
        result = source[here]
        for step in range(1, owners):
            copies[step - 1].wait()
            result = result + arriving[step].astype(F32)
        return result

    if backward:
        back_out[...] = finish(back_total, back_coming, back_copies)
        gate_grad_out[...] = finish(grads, grads_coming, grad_copies)
    if forward:
        hidden_out[...] = (middle_in[...] + finish(total, coming, mix_copies)).astype(BF16)


def expert_stage(mode, layer, number, weights, middle, gates, normed, up):
    owners = lax.axis_size("expert")
    local = weights[0].shape[1]
    forward, backward = "f" in mode, "b" in mode
    tokens = (normed if forward else up).shape[0]
    rows = owners * tokens
    shape = jax.ShapeDtypeStruct
    sems = pltpu.SemaphoreType.DMA
    arguments, specs = list(weights), [any_spec()] * 4
    if forward:
        arguments.append(middle)
    arguments += [gates, normed]
    if backward:
        arguments.append(up)
    specs += [vmem_spec()] * (len(arguments) - 4)
    outs = []
    scratch = [
        pltpu.VMEM((local, MODEL_WIDTH, 2 * FF), BF16),
        pltpu.VMEM((local, FF, MODEL_WIDTH), BF16),
        sems((local,)),
        sems((local,)),
    ]
    pair = [sems((owners,)), sems((owners,))]
    if forward:
        outs += [
            shape((tokens, MODEL_WIDTH), BF16),
            shape((rows, MODEL_WIDTH), BF16),
            shape((rows, LANES), F32),
        ]
        scratch += [pltpu.VMEM((rows, MODEL_WIDTH), BF16), pltpu.VMEM((rows, LANES), F32)] + pair + pair
        scratch += [
            pltpu.VMEM((rows, MODEL_WIDTH), F32),
            pltpu.VMEM((owners, tokens, MODEL_WIDTH), BF16),
            pltpu.VMEM((owners, tokens, MODEL_WIDTH), BF16),
        ] + pair
    if backward:
        outs += [shape((tokens, MODEL_WIDTH), F32), shape((tokens, LANES), F32)]
        scratch += [pltpu.VMEM((rows, MODEL_WIDTH), BF16)] + pair
        scratch += [
            pltpu.VMEM((rows, MODEL_WIDTH), F32),
            pltpu.VMEM((owners, tokens, MODEL_WIDTH), BF16),
            pltpu.VMEM((owners, tokens, MODEL_WIDTH), BF16),
        ] + pair
        scratch += [
            pltpu.VMEM((rows, LANES), F32),
            pltpu.VMEM((owners, tokens, LANES), F32),
            pltpu.VMEM((owners, tokens, LANES), F32),
        ] + pair
    return pl.pallas_call(
        functools.partial(expert_kernel, mode, layer, owners, tokens, local),
        out_shape=tuple(outs),
        in_specs=specs,
        out_specs=tuple(vmem_spec() for _ in outs),
        scratch_shapes=scratch,
        compiler_params=pltpu.CompilerParams(
            collective_id=number, has_side_effects=True, vmem_limit_bytes=VMEM_LIMIT
        ),
        name="experts_" + mode,
    )(*arguments)


def weight_grad_kernel(
    x_ref, up_ref, gate_ref, win_ref, wout_ref, grad_in_ref, grad_out_ref, activated_ref
):
    expert, block = pl.program_id(0), pl.program_id(1)
    plane = lax.axis_index("dp")
    local = pl.num_programs(0)
    mine = lax.axis_index("expert") * local + expert
    slice_in, slice_out = grad_in_ref.shape[0], grad_out_ref.shape[0]
    lane = lane_of(gate_ref.shape)
    gate = jnp.sum(jnp.where(lane == mine, gate_ref[...], 0.0), axis=-1, keepdims=True)
    pair = dot_nn(x_ref[...], win_ref[...])
    gate_part, up_part = pair[:, :FF], pair[:, FF:]
    sigmoid = 1.0 / (1.0 + jnp.exp(-gate_part))
    silu = gate_part * sigmoid
    activated_ref[...] = (silu * up_part * gate).astype(BF16)
    grad_activated = dot_nt(up_ref[...], wout_ref[...]) * gate
    grad_gate = grad_activated * up_part * sigmoid * (1.0 + gate_part * (1.0 - sigmoid))
    grad_up = grad_activated * silu
    grad_pair = jnp.concatenate([grad_gate.astype(BF16), grad_up.astype(BF16)], axis=-1)
    mine_in = x_ref[:, pl.ds(pl.multiple_of(plane * slice_in, LANES), slice_in)]
    mine_out = activated_ref[:, pl.ds(pl.multiple_of(plane * slice_out, LANES), slice_out)]
    term_in = dot_tn(mine_in, grad_pair)
    term_out = dot_tn(mine_out, up_ref[...])

    @pl.when(block == 0)
    def _():
        grad_in_ref[...] = term_in
        grad_out_ref[...] = term_out

    @pl.when(block > 0)
    def _():
        grad_in_ref[...] += term_in
        grad_out_ref[...] += term_out


def weight_grads(x, up, gates, experts_in, experts_out):
    planes = lax.axis_size("dp")
    local = experts_in.shape[1]
    rows = x.shape[0]
    block = 512
    shape = jax.ShapeDtypeStruct
    return pl.pallas_call(
        weight_grad_kernel,
        grid=(local, rows // block),
        out_shape=(
            shape((local, MODEL_WIDTH // planes, 2 * FF), F32),
            shape((local, FF // planes, MODEL_WIDTH), F32),
        ),
        in_specs=[
            pl.BlockSpec((block, MODEL_WIDTH), lambda e, b: (b, 0)),
            pl.BlockSpec((block, MODEL_WIDTH), lambda e, b: (b, 0)),
            pl.BlockSpec((block, LANES), lambda e, b: (b, 0)),
            pl.BlockSpec((None, None, MODEL_WIDTH, 2 * FF), lambda e, b: (0, e, 0, 0)),
            pl.BlockSpec((None, None, FF, MODEL_WIDTH), lambda e, b: (0, e, 0, 0)),
        ],
        out_specs=(
            pl.BlockSpec((None, MODEL_WIDTH // planes, 2 * FF), lambda e, b: (e, 0, 0)),
            pl.BlockSpec((None, FF // planes, MODEL_WIDTH), lambda e, b: (e, 0, 0)),
        ),
        scratch_shapes=[pltpu.VMEM((block, FF), BF16)],
        compiler_params=pltpu.CompilerParams(vmem_limit_bytes=VMEM_LIMIT),
        name="weight_grads",
    )(x, up, gates, experts_in, experts_out)


def rotated_blocks(block, axis):
    length = lax.axis_size(axis)
    blocks = [block]
    for step in range(1, length):
        blocks.append(lax.ppermute(block, axis, [(i, (i + step) % length) for i in range(length)]))
    return jnp.stack(blocks)


def shards(layer_input, cotangent, positions, routes, gain_one, attn_in, attn_out, gain_two, router,
           experts_in, experts_out):
    section = lax.axis_index("section")
    first = section == 0
    planes = lax.axis_size("dp")
    owners = lax.axis_size("expert")
    own = lax.axis_index("expert")
    tokens = layer_input.shape[1]

    def swap(values):
        return lax.ppermute(values, "section", [(0, 1), (1, 0)])

    def layered(mine, other):
        return jnp.stack([jnp.where(first, mine, other), jnp.where(first, other, mine)])

    def both(mine):
        return layered(mine, swap(mine))

    win_other, wout_other = swap(experts_in), swap(experts_out)
    weights = (experts_in, win_other, experts_out, wout_other)
    win, wout = gather_weights(attn_in, attn_out)
    gains = both(jnp.concatenate([gain_one, gain_two], axis=0))
    gains_one, gains_two = gains[:, 0:1], gains[:, 1:2]
    routers = both(jnp.pad(router[0], ((0, 0), (0, LANES - EXPERTS))))

    pick = functools.partial(lax.dynamic_index_in_dim, axis=0, keepdims=False)
    x = pick(layer_input, section)
    up = pick(cotangent, section)
    place = pick(positions, section)
    choices = layered(pick(routes[0], section), swap(pick(routes[0], 1 - section)))
    hot = jnp.sum(
        (choices[..., None] == jnp.arange(LANES, dtype=jnp.int32)).astype(F32), axis=2
    )
    lane = jnp.arange(LANES)
    frequency = jnp.power(rotary_base, -((lane % HALF).astype(F32) * (2.0 / HEAD_SIZE)))
    angles = place.astype(F32)[:, None] * frequency[None, :]
    cosine = jnp.cos(angles)
    sine = jnp.where(lane % HEAD_SIZE < HALF, -1.0, 1.0) * jnp.sin(angles)

    def ahead(layer, entering):
        return attention_forward(layer, entering, gains_one, win, wout, gains_two, routers, hot, cosine, sine)

    def behind(layer, entering, kept, upstream, back, gate_grads):
        return attention_backward(
            layer, entering, gains_one, win, wout, gains_two, routers, cosine, sine, kept, upstream, back, gate_grads
        )

    middle0, normed0, gates0, *kept0 = ahead(0, x)
    hidden0, plane0, plane_gates0 = expert_stage("f", 0, 1, weights, middle0, gates0, normed0, None)
    middle1, normed1, gates1, *kept1 = ahead(1, hidden0)
    hidden1, plane1, plane_gates1, back1, gate_grads1 = expert_stage(
        "fb", 1, 2, weights, middle1, gates1, normed1, up
    )
    grad1, projected1, low1, first1, logits1, gain_grads1 = behind(
        1, hidden0, (middle1, gates1, *kept1), up, back1, gate_grads1
    )
    back0, gate_grads0 = expert_stage("b", 0, 3, weights, None, plane_gates0, plane0, grad1)
    grad0, projected0, low0, first0, logits0, gain_grads0 = behind(
        0, x, (middle0, gates0, *kept0), grad1, back0, gate_grads0
    )

    def regroup(value0, value1):
        mine = jnp.where(first, value0, value1)
        return mine, swap(jnp.where(first, value1, value0))

    def ordered(pair):
        mine, other = pair
        return jnp.stack([jnp.where(first, mine, other), jnp.where(first, other, mine)])

    hidden = ordered(regroup(hidden0, hidden1))[None]
    input_grad = ordered(regroup(grad0, grad1))[None]

    high0, high1 = gates0.astype(BF16), gates1.astype(BF16)
    rest0, rest1 = (gates0 - high0.astype(F32)).astype(BF16), (gates1 - high1.astype(F32)).astype(BF16)
    pack0 = jnp.concatenate([normed0, grad1, logits0, high0, rest0], axis=-1)
    pack1 = jnp.concatenate([normed1, up, logits1, high1, rest1], axis=-1)
    pack = jnp.concatenate(regroup(pack0, pack1), axis=0)
    everything = rotated_blocks(rotated_blocks(pack, "dp"), "expert").reshape(-1, pack.shape[1])
    every_x = everything[:, :MODEL_WIDTH]
    every_up = everything[:, MODEL_WIDTH : 2 * MODEL_WIDTH]
    small = everything[:, 2 * MODEL_WIDTH :].reshape(-1, 3, LANES)
    every_gate = small[:, 1].astype(F32) + small[:, 2].astype(F32)
    grad_experts_in, grad_experts_out = weight_grads(every_x, every_up, every_gate, experts_in, experts_out)
    grad_router = dot_tn(every_x, small[:, 0])[:, :EXPERTS]

    factors0 = jnp.concatenate([projected0, low0, first0, kept0[3]], axis=-1)
    factors1 = jnp.concatenate([projected1, low1, first1, kept1[3]], axis=-1)
    factors = jnp.concatenate(regroup(factors0, factors1), axis=0)
    around = rotated_blocks(factors, "expert").reshape(-1, factors.shape[1])
    part = MODEL_WIDTH // (planes * owners)

    def mine_of(values):
        blocks = values.reshape(-1, planes, owners, part)
        return lax.dynamic_index_in_dim(blocks, own, 2, keepdims=False).reshape(-1, planes * part)

    start = PROJECTED + MODEL_WIDTH
    grad_in = dot_tn(mine_of(around[:, start : start + MODEL_WIDTH]), around[:, :PROJECTED])
    grad_out = dot_tn(mine_of(around[:, start + MODEL_WIDTH :]), around[:, PROJECTED:start])
    partial = jnp.concatenate([grad_in, grad_out], axis=-1).reshape(planes, part, -1)
    plane = lax.axis_index("dp")
    total = pick(partial, plane)
    for step in range(1, planes):
        leaving = pick(partial, (plane + step) % planes).astype(BF16)
        pairs = [(i, (i + step) % planes) for i in range(planes)]
        total = total + lax.ppermute(leaving, "dp", pairs).astype(F32)
    grad_attn_in, grad_attn_out = total[:, :PROJECTED], total[:, PROJECTED:]

    gain_mine, gain_other = regroup(gain_grads0[:2], gain_grads1[:2])
    gain_sums = lax.psum(gain_mine + gain_other, ("dp", "expert"))
    return (
        hidden,
        input_grad,
        gain_sums[0:1],
        grad_attn_in[None],
        grad_attn_out[None],
        gain_sums[1:2],
        grad_router[None],
        grad_experts_in[None],
        grad_experts_out[None],
    )


def solution(mesh):
    in_specs = (
        P(None, ("dp", "expert"), None),
        P(None, ("dp", "expert"), None),
        P(None, ("dp", "expert")),
        P("section", None, ("dp", "expert"), None),
        P("section", None),
        P("section", "dp", None),
        P("section", "dp", None),
        P("section", None),
        P("section", None, None),
        P("section", "expert", None, None),
        P("section", "expert", None, None),
    )
    out_specs = (
        P("section", None, ("dp", "expert"), None),
        P("section", None, ("dp", "expert"), None),
        P("section", None),
        P("section", ("dp", "expert"), None),
        P("section", ("dp", "expert"), None),
        P("section", None),
        P("section", None, None),
        P("section", "expert", "dp", None),
        P("section", "expert", "dp", None),
    )
    return jax.shard_map(shards, mesh=mesh, in_specs=in_specs, out_specs=out_specs, check_vma=False)
```

time: 1610 us -> 576 us (0.36)
  waiting for transfers between devices: 799 us -> 91.8 us
  matrix products: 364 us -> 9.14 us
  Pallas kernels: 0 us -> 327 us
  local copies, waits for them, and re-layouts: 150 us -> 30.9 us
  starting transfers between devices: 74.8 us -> 15.5 us
  blocking collectives: 130 us -> 74.1 us
  other arithmetic: 64.4 us -> 24.7 us
  between operations: 17.7 us -> 1.47 us
    reduce_scatter x4 -> x0, waiting for transfers between devices: 402 us -> none  [the longest x1 180 us: shards(): lax.psum_scatter(delta_attn_in, ('dp', 'expert'), scatter_dimension=0, ti...]
    dot_general x108 -> x3, matrix products: 364 us -> 9.14 us  [dot_tn(): lax.dot_general(a, b, (((0,), (0,)), ((), ())), preferred_element_type=F32)]
    pallas_call x0 -> x9, Pallas kernels: none -> 327 us  [the longest x3 113 us: expert_stage(): pl.pallas_call(functools.partial(expert_kernel, mode, layer, owners, toke...]
    all_to_all x15 -> x0, waiting for transfers between devices: 173 us -> none  [the longest x6 79.5 us: layer_forward(): lax.all_to_all(produced, 'expert', split_axis=1, concat_axis=1, tiled=True)]
    all_gather x2 -> x0, waiting for transfers between devices: 117 us -> none  [the longest x1 76.9 us: shards(): lax.all_gather(attn_in[0], 'dp', axis=0, tiled=True)]
    psum x1 -> x0, waiting for transfers between devices: 105 us -> none  [shards(): lax.psum((delta_gain_first, delta_gain_second, delta_router), ('dp', 'exp...]
    ppermute x4 -> x22, waiting for transfers between devices: 0.5 us -> 91.8 us  [the longest x9 61.7 us: rotated_blocks(): lax.ppermute(block, axis, [(i, (i + step) % length) for i in range(length)])]
    all_to_all x3 -> x0, blocking collectives: 87.1 us -> none  [layer_forward(): lax.all_to_all(outgoing, 'expert', split_axis=1, concat_axis=1, tiled=True)]
  transfers between devices with their start and end apart: 26 -> 22, of which waited for: 21 -> 10; matrix products, arithmetic and copies ran while one was open for 24% -> 7% of each run, Pallas kernels for 0% -> 17%
where the time goes in v1:
time: 576 us; the launch traced here: 575 us
  Pallas kernels  327 us (57%)
  waiting for transfers between devices  91.8 us (16%)
  blocking collectives  74.1 us (13%)
  local copies, waits for them, and re-layouts  30.9 us (5%)
  other arithmetic  24.7 us (4%)
  starting transfers between devices  15.5 us (3%)
  matrix products  9.14 us (2%)
    pallas_call x3, Pallas kernels, expert_stage(): pl.pallas_call(functools.partial(expert_kernel, mode, layer, owners, toke...  113 us
    pallas_call x1, Pallas kernels, gather_weights(): pl.pallas_call(functools.partial(gather_kernel, planes, owners, rows), ou...  93.9 us
    pallas_call x1, Pallas kernels, weight_grads(): pl.pallas_call(weight_grad_kernel, grid=(local, rows // block), out_shape...  91.1 us
    psum x1, blocking collectives, shards(): gain_sums = lax.psum(gain_mine + gain_other, ('dp', 'expert'))  74.1 us
    ppermute x9, waiting for transfers between devices, rotated_blocks(): lax.ppermute(block, axis, [(i, (i + step) % length) for i in range(length)])  61.7 us
    ppermute x3, waiting for transfers between devices, shards(): total = total + lax.ppermute(leaving, 'dp', pairs).astype(F32)  27.5 us
    unnamed x72, local copies, waits for them, and re-layouts  17.3 us
    pallas_call x2, Pallas kernels, attention_backward(): pl.pallas_call(functools.partial(attention_backward_kernel, layer), out_s...  15.9 us
  transfers between devices with their start and end apart: 22, of which 10 were waited for; matrix products, arithmetic and copies ran while one was open for 7% of the time, Pallas kernels for 17%

profile of v1, /device:TPU:0, one launch (start us, length us, event | category | flops | bytes accessed | tf_op | source)
XLA Modules:
  0.0 574.7 jit_solution(1654411574689561795)
XLA Ops:
  7.0 93.9 %gather_weights.1 = (bf16[2,1024,2048]{2,1,0:T(8,128)(2,1)}, bf16[2,1024,1024]{2,1,0:T(8,128)(2,1)}) custom-call(bf16[1,256,2048]{2,1,0:T(8,128)(2,1)} %in_ref.1, bf16[1,256,1024]{2,1,0:T(8,128)(2,1)} %out_ref.1), custom_call_target="tpu_custom_call" | custom-call | tf_op jit(solution)/shard_map/gather_weights/pallas_call | solution.py:158
  104.2 6.3 %attention_forward.2 = (f32[64,1024]{1,0:T(8,128)}, bf16[64,1024]{1,0:T(8,128)(2,1)}, f32[64,128]{1,0:T(8,128)}, bf16[64,1024]{1,0:T(8,128)(2,1)}, bf16[64,1024]...) custom-call(bf16[64,1024]{1,0:T(8,128)(2,1)} %dynamic-slice_bitcast_fusion.1.x_ref, ...), custom_call_target="tpu_custom_call" | custom-call | tf_op jit(solution)/shard_map/attention_forward/pallas_call | solution.py:256
  111.5 29.7 %experts_f.1 = (bf16[64,1024]{1,0:T(8,128)(2,1)}, bf16[256,1024]{1,0:T(8,128)(2,1)}, f32[256,128]{1,0:T(8,128)}) custom-call(bf16[1,8,1024,1024]{3,2,1,0:T(8,128)(2,1)} %win_ref.1, bf16[1,8,1024,1024]{3,2,1,0:T(8,128)(2,1)} %collective-permute-done.refs_1_, bf16[1,8,512,1024]{3,2,1,0:T(8,128)(2,1)} %wout_ref.1, ...), custom_call_target="tpu_custom_call" | custom-call | tf_op jit(solution)/shard_map/experts_f/pallas_call | solution.py:600
  141.2 6.4 %attention_forward.3 = (f32[64,1024]{1,0:T(8,128)}, bf16[64,1024]{1,0:T(8,128)(2,1)}, f32[64,128]{1,0:T(8,128)}, bf16[64,1024]{1,0:T(8,128)(2,1)}, bf16[64,1024]...) custom-call(bf16[64,1024]{1,0:T(8,128)(2,1)} %get-tuple-element.54.x_ref, ...), custom_call_target="tpu_custom_call" | custom-call | tf_op jit(solution)/shard_map/attention_forward/pallas_call | solution.py:256
  149.2 51.0 %experts_fb.1 = (bf16[64,1024]{1,0:T(8,128)(2,1)}, bf16[256,1024]{1,0:T(8,128)(2,1)}, f32[256,128]{1,0:T(8,128)}, f32[64,1024]{1,0:T(8,128)}, f32[64,128]{1,0:T(8,128)}) custom-call(bf16[1,8,1024,1024]{3,2,1,0:T(8,128)(2,1)} %win_ref.1, bf16[1,8,1024,1024]{3,2,1,0:T(8,128)(2,1)} %collective-permute-done.refs_1_, bf16[1,8,512,1024]{3,2,1,0:T(8,128)(2,1)} %wout_ref.1, ...), custom_call_target="tpu_custom_call" | custom-call | tf_op jit(solution)/shard_map/experts_fb/pallas_call | solution.py:600
  200.2 7.9 %attention_backward.2 = (bf16[64,1024]{1,0:T(8,128)(2,1)}, bf16[64,2048]{1,0:T(8,128)(2,1)}, bf16[64,1024]{1,0:T(8,128)(2,1)}, bf16[64,1024]{1,0:T(8,128)(2,1)},...) custom-call(bf16[64,1024]{1,0:T(8,128)(2,1)} %get-tuple-element.54.x_ref, f32[1,1024]{1,0:T(1,128)} %get-tuple-element.128.gain_one_ref, ...), custom_call_target="tpu_custom_call" | custom-call | tf_op jit(solution)/shard_map/attention_backward/pallas_call | solution.py:365
  208.9 32.6 %experts_b.1 = (f32[64,1024]{1,0:T(8,128)}, f32[64,128]{1,0:T(8,128)}) custom-call(bf16[1,8,1024,1024]{3,2,1,0:T(8,128)(2,1)} %win_ref.1, bf16[1,8,1024,1024]{3,2,1,0:T(8,128)(2,1)} %collective-permute-done.refs_1_, bf16[1,8,512,1024]{3,2,1,0:T(8,128)(2,1)} %wout_ref.1, bf16[1,8,512,1024]{3,2,1,0:T(8,128)(2,1)} %collective-permute-done.1.refs_3_, ...), custom_call_target="tpu_custom_call" | custom-call | tf_op jit(solution)/shard_map/experts_b/pallas_call | solution.py:600
  241.6 8.0 %attention_backward.3 = (bf16[64,1024]{1,0:T(8,128)(2,1)}, bf16[64,2048]{1,0:T(8,128)(2,1)}, bf16[64,1024]{1,0:T(8,128)(2,1)}, bf16[64,1024]{1,0:T(8,128)(2,1)},...) custom-call(bf16[64,1024]{1,0:T(8,128)(2,1)} %dynamic-slice_bitcast_fusion.1.x_ref, ...), custom_call_target="tpu_custom_call" | custom-call | tf_op jit(solution)/shard_map/attention_backward/pallas_call | solution.py:365
  253.9 1.8 fusion.20
  255.7 2.3 collective-permute-start.9
  262.1 2.7 collective-permute-start.17
  264.7 7.0 %collective-permute-done.16 = bf16[128,2432]{1,0:T(8,128)(2,1)S(1)} collective-permute-done((bf16[128,2432]{1,0:T(8,128)(2,1)S(1)}, bf16[128,2432]{1,0:T(8,128)(2,1)S(1)}, u32[]{:S(2)}, u32[]{:S(2)}) %collective-permute-start.16) | collective-permute-done | bytes 622624 | tf_op jit(solution)/shard_map/ppermute | solution.py:682
  271.8 2.4 collective-permute-start.18
  275.6 74.1 %psum.7 = f32[2,1024]{1,0:T(2,128)S(1)} all-reduce(f32[2,1024]{1,0:T(2,128)S(1)} %select_add_fusion), channel_id=1, replica_groups=mesh['section'=2,'dp'=4,'expert'=4] {'dp','expert'}, use_global_device_ids=true, to_apply=%region_1.2 | all-reduce | flops 2048 | bytes 16384 | tf_op jit(solution)/shard_map/psum | solution.py:794
  350.7 2.9 fusion.22
  353.8 2.9 collective-permute-start.21
  356.7 3.2 pad_maximum_fusion.1
  359.9 2.3 copy-done.3
  362.2 1.5 fusion.24
  363.7 2.3 copy.36
  367.0 3.7 fusion
  370.7 2.3 copy.37
  374.1 1.7 fusion.2
  378.4 11.9 %collective-permute-done.12 = bf16[64,3072]{1,0:T(8,128)(2,1)S(1)} collective-permute-done((bf16[64,3072]{1,0:T(8,128)(2,1)S(1)}, bf16[64,3072]{1,0:T(8,128)(2,1)S(1)}, u32[]{:S(2)}, u32[]{:S(2)}) %collective-permute-start.12) | collective-permute-done | bytes 393248 | tf_op jit(solution)/shard_map/ppermute | solution.py:790
  391.8 14.2 %collective-permute-done.13 = bf16[64,3072]{1,0:T(8,128)(2,1)S(1)} collective-permute-done((bf16[64,3072]{1,0:T(8,128)(2,1)S(1)}, bf16[64,3072]{1,0:T(8,128)(2,1)S(1)}, u32[]{:S(2)}, u32[]{:S(2)}) %collective-permute-start.13) | collective-permute-done | bytes 393248 | tf_op jit(solution)/shard_map/ppermute | solution.py:790
  409.1 2.8 collective-permute-done.19
  411.8 51.9 %collective-permute-done.20 = bf16[4,128,2432]{2,1,0:T(8,128)(2,1)} collective-permute-done((bf16[4,128,2432]{2,1,0:T(8,128)(2,1)}, bf16[4,128,2432]{2,1,0:T(8,128)(2,1)}, u32[]{:S(2)}, u32[]{:S(2)}) %collective-permute-start.20) | collective-permute-done | bytes 2490400 | tf_op jit(solution)/shard_map/ppermute | solution.py:682
  463.8 5.5 pad_maximum_fusion
  469.5 3.7 copy-done.2
  473.2 3.9 fusion.23
  478.6 3.8 convolution_bitcast_fusion
  483.5 91.1 %weight_grads.1 = (f32[8,256,1024]{2,1,0:T(8,128)}, f32[8,128,1024]{2,1,0:T(8,128)}) custom-call(bf16[2048,1024]{1,0:T(8,128)(2,1)} %get-tuple-element.92.x_ref, bf16[2048,1024]{1,0:T(8,128)(2,1)} %get-tuple-element.91.up_ref, f32[2048,128]{1,0:T(8,128)} %add_bitcast_fusion.gate_ref, bf16[1,8,1024,1024]{3,2,1,0:T(8,128)(2,1)} %win_ref.1, ...), custom_call_target="tpu_custom_call" | custom-call | tf_op jit(solution)/shard_map/weight_grads/pallas_call | solution.py:654
  (147 shorter events, 35.4 us)
Async XLA Ops:
  0.7 102.0 %copy-start.26 = (f32[1,1024]{1,0:T(1,128)S(1)}, f32[1,1024]{1,0:T(1,128)}, u32[]{:S(2)}) copy-start(f32[1,1024]{1,0:T(1,128)} %param.15) | copy-start | bytes 12292
  0.7 102.0 %copy-start.25 = (f32[1,1024]{1,0:T(1,128)S(1)}, f32[1,1024]{1,0:T(1,128)}, u32[]{:S(2)}) copy-start(f32[1,1024]{1,0:T(1,128)} %param.18) | copy-start | bytes 12292
  0.7 110.8 %collective-permute-start = (bf16[1,8,1024,1024]{3,2,1,0:T(8,128)(2,1)}, bf16[1,8,1024,1024]{3,2,1,0:T(8,128)(2,1)}, u32[]{:S(2)}, u32[]{:S(2)}) collective-permute-start(bf16[1,8,1024,1024]{3,2,1,0:T(8,128)(2,1)} %win_ref.1), channel_id=1, source_target_pairs={{0,16},{16,0},{1,17},{17,1},{2,18},{18,2},{3,19},{19,3},{4,20},{20... | collective-permute-start | bytes 50331656 | tf_op jit(solution)/shard_map/ppermute | solution.py:696
  1.2 110.2 %collective-permute-start.1 = (bf16[1,8,512,1024]{3,2,1,0:T(8,128)(2,1)}, bf16[1,8,512,1024]{3,2,1,0:T(8,128)(2,1)}, u32[]{:S(2)}, u32[]{:S(2)}) collective-permute-start(bf16[1,8,512,1024]{3,2,1,0:T(8,128)(2,1)} %wout_ref.1), channel_id=1, source_target_pairs={{0,16},{16,0},{1,17},{17,1},{2,18},{18,2},{3,19},{19,3},{4,20},{20... | collective-permute-start | bytes 25165832 | tf_op jit(solution)/shard_map/ppermute | solution.py:696
  2.0 99.0 %collective-permute-start.4 = (s32[64,8]{0,1:T(8,128)S(1)}, s32[64,8]{0,1:T(8,128)S(1)}, u32[]{:S(2)}, u32[]{:S(2)}) collective-permute-start(s32[64,8]{0,1:T(8,128)S(1)} %dynamic-slice_bitcast_fusion.2), channel_id=1, source_target_pairs={{0,16},{16,0},{1,17},{17,1},{2,18},{18,2},{3,19},{19,3},{4,20},{20... | collective-permute-start | bytes 6152 | tf_op jit(solution)/shard_map/ppermute | solution.py:696
  3.1 99.5 %collective-permute-start.2 = (f32[2,1024]{1,0:T(2,128)S(1)}, f32[2,1024]{1,0:T(2,128)S(1)}, u32[]{:S(2)}, u32[]{:S(2)}) collective-permute-start(f32[2,1024]{1,0:T(2,128)S(1)} %pad_maximum_fusion.6), channel_id=1, source_target_pairs={{0,16},{16,0},{1,17},{17,1},{2,18},{18,2},{3,19},{19,3},{4,20},{20... | collective-permute-start | bytes 24584 | tf_op jit(solution)/shard_map/ppermute | solution.py:696
  4.3 99.0 %collective-permute-start.3 = (bf16[1024,128]{1,0:T(8,128)(2,1)S(1)}, bf16[1024,128]{1,0:T(8,128)(2,1)S(1)}, u32[]{:S(2)}, u32[]{:S(2)}) collective-permute-start(bf16[1024,128]{1,0:T(8,128)(2,1)S(1)} %pad.4), channel_id=1, source_target_pairs={{0,16},{16,0},{1,17},{17,1},{2,18},{18,2},{3,19},{19,3},{4,20},{20... | collective-permute-start | bytes 786440 | tf_op jit(solution)/shard_map/ppermute | solution.py:696
  241.6 9.7 %copy-start.17 = (bf16[64,2048]{1,0:T(8,128)(2,1)S(1)}, bf16[64,2048]{1,0:T(8,128)(2,1)}, u32[]{:S(2)}) copy-start(bf16[64,2048]{1,0:T(8,128)(2,1)} %get-tuple-element.82) | copy-start | bytes 786436
  241.6 9.7 %copy-start.21 = (bf16[64,1024]{1,0:T(8,128)(2,1)S(1)}, bf16[64,1024]{1,0:T(8,128)(2,1)}, u32[]{:S(2)}) copy-start(bf16[64,1024]{1,0:T(8,128)(2,1)} %get-tuple-element.83) | copy-start | bytes 393220
  241.6 9.7 %copy-start.20 = (bf16[64,1024]{1,0:T(8,128)(2,1)S(1)}, bf16[64,1024]{1,0:T(8,128)(2,1)}, u32[]{:S(2)}) copy-start(bf16[64,1024]{1,0:T(8,128)(2,1)} %get-tuple-element.84) | copy-start | bytes 393220
  241.6 9.7 %copy-start.12 = (bf16[64,1024]{1,0:T(8,128)(2,1)S(1)}, bf16[64,1024]{1,0:T(8,128)(2,1)}, u32[]{:S(2)}) copy-start(bf16[64,1024]{1,0:T(8,128)(2,1)} %get-tuple-element.67.attended_ref) | copy-start | bytes 393220
  251.2 1.7 collective-permute-start.15
  251.6 22.5 %copy-start.6 = (bf16[64,1024]{1,0:T(8,128)(2,1)S(1)}, bf16[64,1024]{1,0:T(8,128)(2,1)}, u32[]{:S(2)}) copy-start(bf16[64,1024]{1,0:T(8,128)(2,1)} %get-tuple-element.54.x_ref) | copy-start | bytes 393220
  251.6 22.5 %copy-start.14 = (bf16[64,1024]{1,0:T(8,128)(2,1)S(1)}, bf16[64,1024]{1,0:T(8,128)(2,1)}, u32[]{:S(2)}) copy-start(bf16[64,1024]{1,0:T(8,128)(2,1)} %get-tuple-element.58) | copy-start | bytes 393220
  251.7 2.3 collective-permute-start.8
  253.0 18.8 %collective-permute-start.16 = (bf16[128,2432]{1,0:T(8,128)(2,1)S(1)}, bf16[128,2432]{1,0:T(8,128)(2,1)S(1)}, u32[]{:S(2)}, u32[]{:S(2)}) collective-permute-start(bf16[128,2432]{1,0:T(8,128)(2,1)S(1)} %get-tuple-element.108), channel_id=1, source_target_pairs={{0,4},{4,8},{8,12},{12,0},{1,5},{5,9},{9,13},{13,1},{2,6},{6,10},{... | collective-permute-start | bytes 1867784 | tf_op jit(solution)/shard_map/ppermute | solution.py:682
  255.7 97.9 %collective-permute-start.9 = (bf16[128,5120]{1,0:T(8,128)(2,1)}, bf16[128,5120]{1,0:T(8,128)(2,1)}, u32[]{:S(2)}, u32[]{:S(2)}) collective-permute-start(bf16[128,5120]{1,0:T(8,128)(2,1)} %get-tuple-element.104), channel_id=1, source_target_pairs={{0,1},{1,2},{2,3},{3,0},{4,5},{5,6},{6,7},{7,4},{8,9},{9,10},{10,1... | collective-permute-start | bytes 3932168 | tf_op jit(solution)/shard_map/ppermute | solution.py:682
  258.0 95.8 %collective-permute-start.10 = (bf16[128,5120]{1,0:T(8,128)(2,1)}, bf16[128,5120]{1,0:T(8,128)(2,1)}, u32[]{:S(2)}, u32[]{:S(2)}) collective-permute-start(bf16[128,5120]{1,0:T(8,128)(2,1)} %get-tuple-element.104), channel_id=1, source_target_pairs={{0,2},{1,3},{2,0},{3,1},{4,6},{5,7},{6,4},{7,5},{8,10},{9,11},{10,... | collective-permute-start | bytes 3932168 | tf_op jit(solution)/shard_map/ppermute | solution.py:682
  259.4 97.2 %collective-permute-start.11 = (bf16[128,5120]{1,0:T(8,128)(2,1)}, bf16[128,5120]{1,0:T(8,128)(2,1)}, u32[]{:S(2)}, u32[]{:S(2)}) collective-permute-start(bf16[128,5120]{1,0:T(8,128)(2,1)} %get-tuple-element.104), channel_id=1, source_target_pairs={{0,3},{1,0},{2,1},{3,2},{4,7},{5,4},{6,5},{7,6},{8,11},{9,8},{10,9... | collective-permute-start | bytes 3932168 | tf_op jit(solution)/shard_map/ppermute | solution.py:682
  260.9 1.2 collective-permute-start.7
  262.1 87.6 %collective-permute-start.17 = (bf16[128,2432]{1,0:T(8,128)(2,1)S(1)}, bf16[128,2432]{1,0:T(8,128)(2,1)S(1)}, u32[]{:S(2)}, u32[]{:S(2)}) collective-permute-start(bf16[128,2432]{1,0:T(8,128)(2,1)S(1)} %get-tuple-element.108), channel_id=1, source_target_pairs={{0,8},{4,12},{8,0},{12,4},{1,9},{5,13},{9,1},{13,5},{2,10},{6,14},... | collective-permute-start | bytes 1867784 | tf_op jit(solution)/shard_map/ppermute | solution.py:682
  271.8 78.0 %copy-start.8 = (bf16[128,2432]{1,0:T(8,128)(2,1)}, bf16[128,2432]{1,0:T(8,128)(2,1)S(1)}, u32[]{:S(2)}) copy-start(bf16[128,2432]{1,0:T(8,128)(2,1)S(1)} %collective-permute-done.16) | copy-start | bytes 1867780
  271.8 78.0 %collective-permute-start.18 = (bf16[128,2432]{1,0:T(8,128)(2,1)S(1)}, bf16[128,2432]{1,0:T(8,128)(2,1)S(1)}, u32[]{:S(2)}, u32[]{:S(2)}) collective-permute-start(bf16[128,2432]{1,0:T(8,128)(2,1)S(1)} %get-tuple-element.108), channel_id=1, source_target_pairs={{0,12},{4,0},{8,4},{12,8},{1,13},{5,1},{9,5},{13,9},{2,14},{6,2},{... | collective-permute-start | bytes 1867784 | tf_op jit(solution)/shard_map/ppermute | solution.py:682
  349.7 27.3 %collective-permute-start.6 = (bf16[64,1024]{1,0:T(8,128)(2,1)}, bf16[64,1024]{1,0:T(8,128)(2,1)}, u32[]{:S(2)}, u32[]{:S(2)}) collective-permute-start(bf16[64,1024]{1,0:T(8,128)(2,1)} %get-tuple-element.118), channel_id=1, source_target_pairs={{0,16},{16,0},{1,17},{17,1},{2,18},{18,2},{3,19},{19,3},{4,20},{20... | collective-permute-start | bytes 393224 | tf_op jit(solution)/shard_map/ppermute | solution.py:696
  353.7 58.2 %collective-permute-start.19 = (bf16[4,128,2432]{2,1,0:T(8,128)(2,1)}, bf16[4,128,2432]{2,1,0:T(8,128)(2,1)}, u32[]{:S(2)}, u32[]{:S(2)}) collective-permute-start(bf16[4,128,2432]{2,1,0:T(8,128)(2,1)} %get-tuple-element.99), channel_id=1, source_target_pairs={{0,1},{1,2},{2,3},{3,0},{4,5},{5,6},{6,7},{7,4},{8,9},{9,10},{10,1... | collective-permute-start | bytes 7471112 | tf_op jit(solution)/shard_map/ppermute | solution.py:682
  353.7 110.1 %collective-permute-start.20 = (bf16[4,128,2432]{2,1,0:T(8,128)(2,1)}, bf16[4,128,2432]{2,1,0:T(8,128)(2,1)}, u32[]{:S(2)}, u32[]{:S(2)}) collective-permute-start(bf16[4,128,2432]{2,1,0:T(8,128)(2,1)} %get-tuple-element.99), channel_id=1, source_target_pairs={{0,2},{1,3},{2,0},{3,1},{4,6},{5,7},{6,4},{7,5},{8,10},{9,11},{10,... | collective-permute-start | bytes 7471112 | tf_op jit(solution)/shard_map/ppermute | solution.py:682
  353.8 110.0 %collective-permute-start.21 = (bf16[4,128,2432]{2,1,0:T(8,128)(2,1)}, bf16[4,128,2432]{2,1,0:T(8,128)(2,1)}, u32[]{:S(2)}, u32[]{:S(2)}) collective-permute-start(bf16[4,128,2432]{2,1,0:T(8,128)(2,1)} %get-tuple-element.99), channel_id=1, source_target_pairs={{0,3},{1,0},{2,1},{3,2},{4,7},{5,4},{6,5},{7,6},{8,11},{9,8},{10,9... | collective-permute-start | bytes 7471112 | tf_op jit(solution)/shard_map/ppermute | solution.py:682
  376.3 14.0 %collective-permute-start.12 = (bf16[64,3072]{1,0:T(8,128)(2,1)S(1)}, bf16[64,3072]{1,0:T(8,128)(2,1)S(1)}, u32[]{:S(2)}, u32[]{:S(2)}) collective-permute-start(bf16[64,3072]{1,0:T(8,128)(2,1)S(1)} %get-tuple-element.95), channel_id=1, source_target_pairs={{0,4},{4,8},{8,12},{12,0},{1,5},{5,9},{9,13},{13,1},{2,6},{6,10},{... | collective-permute-start | bytes 1179656 | tf_op jit(solution)/shard_map/ppermute | solution.py:790
  377.0 1.4 collective-permute-start.5
  378.4 27.6 %collective-permute-start.13 = (bf16[64,3072]{1,0:T(8,128)(2,1)S(1)}, bf16[64,3072]{1,0:T(8,128)(2,1)S(1)}, u32[]{:S(2)}, u32[]{:S(2)}) collective-permute-start(bf16[64,3072]{1,0:T(8,128)(2,1)S(1)} %get-tuple-element.97), channel_id=1, source_target_pairs={{0,8},{4,12},{8,0},{12,4},{1,9},{5,13},{9,1},{13,5},{2,10},{6,14},... | collective-permute-start | bytes 1179656 | tf_op jit(solution)/shard_map/ppermute | solution.py:790
  390.3 17.0 %collective-permute-start.14 = (bf16[64,3072]{1,0:T(8,128)(2,1)S(1)}, bf16[64,3072]{1,0:T(8,128)(2,1)S(1)}, u32[]{:S(2)}, u32[]{:S(2)}) collective-permute-start(bf16[64,3072]{1,0:T(8,128)(2,1)S(1)} %get-tuple-element.96), channel_id=1, source_target_pairs={{0,12},{4,0},{8,4},{12,8},{1,13},{5,1},{9,5},{13,9},{2,14},{6,2},{... | collective-permute-start | bytes 1179656 | tf_op jit(solution)/shard_map/ppermute | solution.py:790
  483.5 91.1 %copy-start.1 = (bf16[2,64,1024]{2,1,0:T(8,128)(2,1)S(1)}, bf16[2,64,1024]{2,1,0:T(8,128)(2,1)}, u32[]{:S(2)}) copy-start(bf16[2,64,1024]{2,1,0:T(8,128)(2,1)} %param.11) | copy-start | bytes 786436
  (18 other events, 74.3 us)

commit v2 on v1

v2 whole, which is shorter than its diff:
```python
import functools

import jax
import jax.numpy as jnp
from jax import lax
from jax.experimental import pallas as pl
from jax.experimental.pallas import tpu as pltpu
from jax.sharding import PartitionSpec as P

MODEL_WIDTH = 1024
QUERY_HEADS = 16
KEY_VALUE_HEADS = 8
HEAD_SIZE = 64
FF = 512
EXPERTS = 32
TOPK = 8

QUERY_WIDTH = QUERY_HEADS * HEAD_SIZE
KEY_WIDTH = KEY_VALUE_HEADS * HEAD_SIZE
PROJECTED = QUERY_WIDTH + 2 * KEY_WIDTH
LANES = 128
HALF = HEAD_SIZE // 2
PACKED = MODEL_WIDTH + LANES

epsilon = 1e-06
rotary_base = 10000.0

F32 = jnp.float32
BF16 = jnp.bfloat16
MESH = pl.DeviceIdType.MESH
VMEM_LIMIT = 62 * 1024 * 1024


def dot_nn(a, b):
    return lax.dot_general(a, b, (((1,), (0,)), ((), ())), preferred_element_type=F32)


def dot_nt(a, b):
    return lax.dot_general(a, b, (((1,), (1,)), ((), ())), preferred_element_type=F32)


def dot_tn(a, b):
    return lax.dot_general(a, b, (((0,), (0,)), ((), ())), preferred_element_type=F32)


def row_scale(values):
    return lax.rsqrt(jnp.mean(values * values, axis=-1, keepdims=True) + epsilon)


def norm_back(grad_normed, inputs, scale):
    return scale * grad_normed - inputs * (scale * scale * scale) * jnp.mean(
        grad_normed * inputs, axis=-1, keepdims=True
    )


def lane_of(shape):
    return lax.broadcasted_iota(jnp.int32, shape, 1)


def turned(tile, low):
    return jnp.where(low, pltpu.roll(tile, LANES - HALF, 1), pltpu.roll(tile, HALF, 1))


def two_parts(values):
    high = values.astype(BF16).astype(F32)
    return (high + pltpu.roll(values - high, EXPERTS, 1)).astype(BF16)


def column_of(parts, lane, column):
    wide = parts.astype(F32)
    return jnp.sum(jnp.where((lane == column) | (lane == column + EXPERTS), wide, 0.0), axis=-1, keepdims=True)


def remote(source, target, send, recv, device):
    return pltpu.make_async_remote_copy(
        src_ref=source, dst_ref=target, send_sem=send, recv_sem=recv, device_id=device, device_id_type=MESH
    )


def vmem_spec():
    return pl.BlockSpec(memory_space=pltpu.VMEM)


def any_spec():
    return pl.BlockSpec(memory_space=pl.ANY)


class Names:
    pass


def call(kernel, name, number, inputs, outputs, scratch):
    labels = list(inputs) + list(outputs) + list(scratch)

    def body(*refs):
        names = Names()
        for label, ref in zip(labels, refs):
            setattr(names, label, ref)
        kernel(names)

    results = pl.pallas_call(
        body,
        out_shape=tuple(jax.ShapeDtypeStruct(shape, dtype) for shape, dtype, _ in outputs.values()),
        in_specs=[spec for _, spec in inputs.values()],
        out_specs=tuple(spec for _, _, spec in outputs.values()),
        scratch_shapes=list(scratch.values()),
        compiler_params=pltpu.CompilerParams(
            collective_id=number, has_side_effects=True, vmem_limit_bytes=VMEM_LIMIT
        ),
        name=name,
    )(*[array for array, _ in inputs.values()])
    return dict(zip(outputs, results))


def layers_kernel(planes, owners, tokens, local, slab, r):
    section = lax.axis_index("section")
    plane = lax.axis_index("dp")
    own = lax.axis_index("expert")
    rows = owners * tokens
    part = slab // owners
    here = pl.ds(own * tokens, tokens)
    partner = {"section": 1 - section}

    def planes_to(step):
        return (plane + step) % planes

    def owner_to(step):
        return (own + step) % owners

    barrier = pltpu.get_barrier_semaphore()
    for step in range(1, owners):
        pl.semaphore_signal(barrier, inc=1, device_id={"expert": owner_to(step)}, device_id_type=MESH)
    for step in range(1, planes):
        for target in range(2):
            pl.semaphore_signal(
                barrier, inc=1, device_id={"section": target, "dp": planes_to(step)}, device_id_type=MESH
            )
    pl.semaphore_signal(barrier, inc=1, device_id=partner, device_id_type=MESH)
    pl.semaphore_wait(barrier, owners - 1 + 2 * (planes - 1) + 1)

    unsent = []

    weight_pairs = ((r.attn_in, r.win), (r.attn_out, r.wout))

    def slab_local(layer, which):
        source, full = weight_pairs[which]
        return pltpu.make_async_copy(
            source.at[0], full.at[layer, pl.ds(plane * slab, slab)], r.w_local.at[layer, which]
        )

    def slab_z(layer, which, step):
        source, full = weight_pairs[which]
        return remote(
            source.at[0, pl.ds(own * part, part)],
            full.at[layer, pl.ds(plane * slab + own * part, part)],
            r.wz_send.at[layer, which, step],
            r.wz_recv.at[layer, which, step],
            {"dp": planes_to(step)},
        )

    def slab_plane(layer, which, step, turn):
        full = weight_pairs[which][1]
        origin = planes_to(planes - step)
        block = full.at[layer, pl.ds(origin * slab + own * part, part)]
        return remote(
            block,
            block,
            r.wp_send.at[layer, which, step, turn],
            r.wp_recv.at[layer, which, step, turn],
            {"expert": owner_to(turn)},
        )

    def slab_core(layer, which, step):
        full = weight_pairs[which][1]
        block = full.at[layer, pl.ds(planes_to(planes - step) * slab, slab)]
        return remote(block, block, r.wc_send.at[layer, which, step], r.wc_recv.at[layer, which, step], partner)

    def weights_start(layer, which):
        @pl.when(section == layer)
        def _():
            for step in range(1, planes):
                slab_z(layer, which, step).start()
            slab_local(layer, which).start()

    def weights_spread(layer, which):
        @pl.when(section == layer)
        def _():
            slab_local(layer, which).wait()
            slab_core(layer, which, 0).start()
            for step in range(1, planes):
                slab_z(layer, which, step).wait_recv()
                for turn in range(1, owners):
                    slab_plane(layer, which, step, turn).start()

    def weights_push(layer, which):
        @pl.when(section == layer)
        def _():
            for step in range(1, planes):
                for turn in range(1, owners):
                    slab_plane(layer, which, step, turn).wait_recv()
                slab_core(layer, which, step).start()

    def weights_wait(layer, which):
        @pl.when(section != layer)
        def _():
            for step in range(planes):
                slab_core(layer, which, step).wait_recv()

    def weights_unsent(layer, which):
        @pl.when(section == layer)
        def _():
            for step in range(1, planes):
                slab_z(layer, which, step).wait_send()
                for turn in range(1, owners):
                    slab_plane(layer, which, step, turn).wait_send()
            for step in range(planes):
                slab_core(layer, which, step).wait_send()

    def swap_pair(expert):
        return (
            remote(r.experts_in.at[0, expert], r.other_in.at[expert], r.s_send.at[0, expert], r.s_recv.at[0, expert], partner),
            remote(r.experts_out.at[0, expert], r.other_out.at[expert], r.s_send.at[1, expert], r.s_recv.at[1, expert], partner),
        )

    def load_in(layer, expert):
        mine = pltpu.make_async_copy(r.experts_in.at[0, expert], r.ein.at[expert], r.l_sem.at[0, expert])
        other = pltpu.make_async_copy(r.other_in.at[expert], r.ein.at[expert], r.l_sem.at[0, expert])
        return mine, other

    def load_out(layer, expert):
        target = r.eout.at[pl.ds(expert * FF, FF)]
        mine = pltpu.make_async_copy(r.experts_out.at[0, expert], target, r.l_sem.at[1, expert])
        other = pltpu.make_async_copy(r.other_out.at[expert], target, r.l_sem.at[1, expert])
        return mine, other

    def start_load(make, layer, expert, which, first_use):
        @pl.when(section == layer)
        def _():
            make(layer, expert)[0].start()

        @pl.when(section != layer)
        def _():
            if first_use:
                swap_pair(expert)[which].wait_recv()
            make(layer, expert)[1].start()

    class Spread:
        def __init__(self, source, buffer, index):
            self.copies = [
                remote(source, buffer.at[own], r.a_send.at[index, step], r.a_recv.at[index, step],
                       {"expert": owner_to(step)})
                for step in range(1, owners)
            ]
            self.source, self.buffer = source, buffer

        def start(self):
            for copy in self.copies:
                copy.start()
            self.buffer[own] = self.source[...]

        def wait(self):
            for copy in self.copies:
                copy.wait_recv()
            unsent.extend(self.copies)

    class Reduce:
        def __init__(self, leaving, coming, index, cuts):
            self.leaving, self.coming, self.index, self.cuts = leaving, coming, index, cuts
            self.copies = {
                (cut, step): remote(
                    leaving.at[step - 1, :, pl.ds(*cuts[cut])],
                    coming.at[step - 1, :, pl.ds(*cuts[cut])],
                    r.r_send.at[index, cut, step],
                    r.r_recv.at[index, cut, step],
                    {"expert": owner_to(step)},
                )
                for cut in range(len(cuts))
                for step in range(1, owners)
            }

        def put(self, step, columns, values):
            self.leaving[step - 1, :, columns] = values

        def start(self, cut):
            for step in range(1, owners):
                self.copies[cut, step].start()

        def wait(self):
            for copy in self.copies.values():
                copy.wait()

    class Gather:
        def __init__(self, layer, block, around, target, index):
            self.layer, self.block, self.around, self.target, self.index = layer, block, around, target, index

        def across(self, step):
            return [
                remote(
                    self.block,
                    self.target.at[own, (planes - step) % planes, section],
                    r.g_send.at[self.index, step],
                    r.g_recv.at[self.index, step, section],
                    {"section": self.layer, "dp": planes_to(step)},
                )
            ][0]

        def arrival(self, step, micro):
            return remote(
                self.block,
                self.target.at[own, (planes - step) % planes, micro],
                r.g_send.at[self.index, step],
                r.g_recv.at[self.index, step, micro],
                {"section": self.layer, "dp": planes_to(step)},
            )

        def home_local(self):
            return pltpu.make_async_copy(self.around, self.target.at[:, 0, section], r.g_local.at[self.index])

        def home_remote(self, micro):
            return remote(self.around, self.target.at[:, 0, micro], r.g_send.at[self.index, 0],
                          r.g_recv.at[self.index, 0, 0], partner)

        def inside(self, turn):
            column = self.target.at[own, pl.ds(1, planes - 1)]
            return remote(column, column, r.gp_send.at[self.index, turn], r.gp_recv.at[self.index, turn],
                          {"expert": owner_to(turn)})

        def start(self):
            for step in range(1, planes):
                self.across(step).start()

        def start_home(self):
            @pl.when(section == self.layer)
            def _():
                self.home_local().start()

            @pl.when(section != self.layer)
            def _():
                self.home_remote(section).start()

        def middle(self):
            @pl.when(section == self.layer)
            def _():
                for step in range(1, planes):
                    for micro in range(2):
                        self.arrival(step, micro).wait_recv()
                for turn in range(1, owners):
                    self.inside(turn).start()

        def finish(self):
            for step in range(1, planes):
                self.across(step).wait_send()

            @pl.when(section == self.layer)
            def _():
                self.home_local().wait()
                self.home_remote(1 - section).wait_recv()
                for turn in range(1, owners):
                    self.inside(turn).wait_recv()
                    self.inside(turn).wait_send()

            @pl.when(section != self.layer)
            def _():
                self.home_remote(section).wait_send()

    class SmallGather:
        def __init__(self, layer, block, target, index):
            self.layer, self.block, self.target, self.index = layer, block, target, index

        def local(self):
            return pltpu.make_async_copy(self.block, self.target.at[own, 0, section], r.q_local.at[self.index])

        def across(self, step, micro):
            device = partner if step == 0 else {"section": self.layer, "dp": planes_to(step)}
            return remote(
                self.block,
                self.target.at[own, (planes - step) % planes, micro],
                r.q_send.at[self.index, step],
                r.q_recv.at[self.index, step, micro],
                device,
            )

        def inside(self, turn):
            column = self.target.at[own]
            return remote(column, column, r.qp_send.at[self.index, turn], r.qp_recv.at[self.index, turn],
                          {"expert": owner_to(turn)})

        def start(self):
            for step in range(1, planes):
                self.across(step, section).start()

            @pl.when(section == self.layer)
            def _():
                self.local().start()

            @pl.when(section != self.layer)
            def _():
                self.across(0, section).start()

        def middle(self):
            @pl.when(section == self.layer)
            def _():
                self.local().wait()
                self.across(0, 1 - section).wait_recv()
                for step in range(1, planes):
                    for micro in range(2):
                        self.across(step, micro).wait_recv()
                for turn in range(1, owners):
                    self.inside(turn).start()

        def finish(self):
            for step in range(1, planes):
                self.across(step, section).wait_send()

            @pl.when(section == self.layer)
            def _():
                for turn in range(1, owners):
                    self.inside(turn).wait()

            @pl.when(section != self.layer)
            def _():
                self.across(0, section).wait_send()

    lane = lane_of((tokens, LANES))
    low_half = lane % HEAD_SIZE < HALF
    left = lane < HEAD_SIZE
    pair_lane = lane_of((2 * tokens, LANES))
    causal = lax.broadcasted_iota(jnp.int32, (2 * tokens, tokens), 0) % tokens >= lax.broadcasted_iota(
        jnp.int32, (2 * tokens, tokens), 1
    )
    root = HEAD_SIZE ** (-0.5)

    def stack(tile):
        nothing = jnp.zeros_like(tile)
        return jnp.concatenate([jnp.where(left, tile, nothing), jnp.where(left, nothing, tile)], axis=0)

    def attention_forward(layer, source, early, late):
        cosine, sine = r.cosine[...], r.sine[...]
        residual = source[...].astype(F32)
        normed_one = (residual * row_scale(residual) * r.gains[layer, 0:1]).astype(BF16)
        weights_wait(layer, 0)
        early()
        r.projected[...] = dot_nn(normed_one, r.win[layer])
        for tile in range(QUERY_WIDTH // LANES):
            columns = slice(tile * LANES, (tile + 1) * LANES)
            piece = r.projected[:, columns]
            r.query[layer, :, columns] = (piece * cosine + turned(piece, low_half) * sine).astype(BF16)
        for tile in range(KEY_WIDTH // LANES):
            first = slice(2 * tile * LANES, (2 * tile + 1) * LANES)
            second = slice((2 * tile + 1) * LANES, (2 * tile + 2) * LANES)
            piece = r.projected[:, QUERY_WIDTH + tile * LANES : QUERY_WIDTH + (tile + 1) * LANES]
            piece = piece * cosine + turned(piece, low_half) * sine
            other = pltpu.roll(piece, HEAD_SIZE, 1)
            r.key[layer, :, first] = jnp.where(left, piece, other).astype(BF16)
            r.key[layer, :, second] = jnp.where(left, other, piece).astype(BF16)
            start = QUERY_WIDTH + KEY_WIDTH + tile * LANES
            piece = r.projected[:, start : start + LANES]
            other = pltpu.roll(piece, HEAD_SIZE, 1)
            r.value[layer, :, first] = jnp.where(left, piece, other).astype(BF16)
            r.value[layer, :, second] = jnp.where(left, other, piece).astype(BF16)
        logs = jnp.zeros((2 * tokens, LANES), F32)
        for head in range(KEY_VALUE_HEADS):
            columns = slice(head * LANES, (head + 1) * LANES)
            scores = dot_nt(stack(r.query[layer, :, columns]), r.key[layer, :, columns]) * root
            scores = jnp.where(causal, scores, -1e30)
            top = jnp.max(scores, axis=-1, keepdims=True)
            log_total = top + jnp.log(jnp.sum(jnp.exp(scores - top), axis=-1, keepdims=True))
            logs = jnp.where(pair_lane == head, log_total, logs)
            weights = jnp.exp(scores - log_total).astype(BF16)
            mixed = dot_nn(weights, r.value[layer, :, columns])
            r.attended[layer, :, columns] = jnp.where(left, mixed[:tokens], mixed[tokens:]).astype(BF16)
        r.logs[layer] = logs
        late()
        weights_wait(layer, 1)
        middle = residual + dot_nn(r.attended[layer], r.wout[layer])
        r.middle[layer] = middle
        normed_two = (middle * row_scale(middle) * r.gains[layer, 1:2]).astype(BF16)
        r.packed[layer, :, :MODEL_WIDTH] = normed_two
        logits = dot_nn(normed_two, r.router[layer])
        chosen = r.hot[layer] > 0.0
        top = jnp.max(jnp.where(chosen, logits, -1e30), axis=-1, keepdims=True)
        grown = jnp.where(chosen, jnp.exp(jnp.where(chosen, logits - top, 0.0)), 0.0)
        gates = grown / jnp.sum(grown, axis=-1, keepdims=True)
        r.gates[layer] = gates
        r.packed[layer, :, MODEL_WIDTH:] = two_parts(gates)

    def attention_backward(layer, source, up, back, gate_grads):
        cosine, sine = r.cosine[...], r.sine[...]
        gates = r.gates[layer]
        grad_picked = gates * (gate_grads - jnp.sum(gates * gate_grads, axis=-1, keepdims=True))
        grad_logits = grad_picked.astype(BF16)
        r.grad_logits[layer] = grad_logits
        grad_second = back + dot_nt(grad_logits, r.router[layer])
        middle = r.middle[layer]
        scale_two = row_scale(middle)
        r.gain_grads[layer, 1:2] = jnp.sum(grad_second * middle * scale_two, axis=0, keepdims=True)
        grad_middle = up[...].astype(F32) + norm_back(grad_second * r.gains[layer, 1:2], middle, scale_two)
        low = grad_middle.astype(BF16)
        r.factors[layer, :, PROJECTED : PROJECTED + MODEL_WIDTH] = low
        r.grad_middle[...] = grad_middle
        r.grad_attended[...] = dot_nt(low, r.wout[layer]).astype(BF16)
        logs = r.logs[layer]
        held = []
        for head in range(KEY_VALUE_HEADS):
            columns = slice(head * LANES, (head + 1) * LANES)
            query = stack(r.query[layer, :, columns])
            key, value = r.key[layer, :, columns], r.value[layer, :, columns]
            scores = dot_nt(query, key) * root
            log_total = jnp.sum(jnp.where(pair_lane == head, logs, 0.0), axis=-1, keepdims=True)
            probabilities = jnp.where(causal, jnp.exp(jnp.where(causal, scores - log_total, 0.0)), 0.0)
            grad_tile = stack(r.grad_attended[:, columns])
            delta = jnp.sum(
                grad_tile.astype(F32) * stack(r.attended[layer, :, columns]).astype(F32), axis=-1, keepdims=True
            )
            grad_scores = (probabilities * (dot_nt(grad_tile, value) - delta)).astype(BF16)
            wide = dot_nn(grad_scores, key) * root
            grad_query = jnp.where(left, wide[:tokens], wide[tokens:])
            grad_query = grad_query * cosine - turned(grad_query, low_half) * sine
            r.factors[layer, :, columns] = grad_query.astype(BF16)
            key_grad = dot_tn(grad_scores, query) * root
            value_grad = dot_tn(probabilities.astype(BF16), grad_tile)
            key_grad = key_grad + pltpu.roll(key_grad, HEAD_SIZE, 1)
            value_grad = value_grad + pltpu.roll(value_grad, HEAD_SIZE, 1)
            if head % 2 == 0:
                held = [key_grad, value_grad]
            else:
                piece = jnp.where(left, held[0], key_grad)
                piece = piece * cosine - turned(piece, low_half) * sine
                start = QUERY_WIDTH + head // 2 * LANES
                r.factors[layer, :, start : start + LANES] = piece.astype(BF16)
                start += KEY_WIDTH
                r.factors[layer, :, start : start + LANES] = jnp.where(left, held[1], value_grad).astype(BF16)
        grad_first = dot_nt(r.factors[layer, :, :PROJECTED], r.win[layer])
        residual = source[...].astype(F32)
        scale_one = row_scale(residual)
        normed_one = (residual * scale_one * r.gains[layer, 0:1]).astype(BF16)
        r.factors[layer, :, PROJECTED + MODEL_WIDTH : PROJECTED + 2 * MODEL_WIDTH] = normed_one
        r.factors[layer, :, PROJECTED + 2 * MODEL_WIDTH :] = r.attended[layer]
        r.gain_grads[layer, 0:1] = jnp.sum(grad_first * residual * scale_one, axis=0, keepdims=True)
        return (
            r.grad_middle[...] + norm_back(grad_first * r.gains[layer, 0:1], residual, scale_one)
        ).astype(BF16)

    def place_local(source, target, index):
        return pltpu.make_async_copy(source, target.at[section], r.o_local.at[index])

    def place_remote(source, target, index, micro):
        return remote(source, target.at[micro], r.o_send.at[index], r.o_recv.at[index], partner)

    def place(layer, source, target, index):
        @pl.when(section == layer)
        def _():
            place_local(source, target, index).start()

        @pl.when(section != layer)
        def _():
            place_remote(source, target, index, section).start()

    def placed(layer, source, target, index):
        @pl.when(section == layer)
        def _():
            place_local(source, target, index).wait()
            place_remote(source, target, index, 1 - section).wait_recv()

        @pl.when(section != layer)
        def _():
            place_remote(source, target, index, section).wait_send()

    chunk = min(rows, 256)
    chunks = rows // chunk
    half = MODEL_WIDTH // 2

    def each_chunk(work):
        def one(number, carry):
            work(pl.ds(pl.multiple_of(number * chunk, chunk), chunk), pl.ds(number * (chunk // tokens), chunk // tokens))
            return carry

        if chunks == 1:
            work(pl.ds(0, chunk), pl.ds(0, owners))
        else:
            lax.fori_loop(0, chunks, one, 0)

    def flat(buffer, group, columns):
        values = buffer[group, :, columns]
        return values.reshape(chunk, values.shape[-1])

    model, packing = slice(0, MODEL_WIDTH), slice(MODEL_WIDTH, PACKED)

    def expert_columns(expert):
        return pl.ds(pl.multiple_of(expert * FF, FF), FF)

    def wait_in(expert):
        load_in(0, expert)[0].wait()

    def wait_out(expert):
        load_out(0, expert)[0].wait()

    def gate_of(plane_buffer, group, expert):
        return column_of(flat(plane_buffer, group, packing), lane_of((chunk, LANES)), own * local + expert)

    def backward_terms(expert, span, gate, gate_part, up_part, inner):
        sigmoid = 1.0 / (1.0 + jnp.exp(-gate_part))
        silu = gate_part * sigmoid
        activated = silu * up_part
        gate_grad = jnp.sum(activated * inner, axis=-1, keepdims=True)
        lanes = lane_of((chunk, LANES))
        r.gate_total[span] = jnp.where(lanes == own * local + expert, gate_grad, r.gate_total[span])
        grad_activated = inner * gate
        grad_gate = grad_activated * up_part * sigmoid * (1.0 + gate_part * (1.0 - sigmoid))
        grad_up = grad_activated * silu
        grad_pair = jnp.concatenate([grad_gate.astype(BF16), grad_up.astype(BF16)], axis=-1)
        term = dot_nt(grad_pair, r.ein[expert])

        @pl.when(expert == 0)
        def _():
            r.total[span] = term

        @pl.when(expert > 0)
        def _():
            r.total[span] += term

        return activated

    def mix(reduction):
        for cut in range(2):
            columns = slice(cut * half, (cut + 1) * half)

            def work(span, group):
                r.total[span, columns] = dot_nn(r.activated[span], r.eout[:, columns])

            each_chunk(work)
            for step in range(1, owners):
                reduction.put(
                    step, columns, r.total[pl.ds(owner_to(step) * tokens, tokens), columns].astype(BF16)
                )
            reduction.start(cut)

    def mixed(reduction, result):
        for step in range(1, owners):
            result = result + reduction.coming[step - 1].astype(F32)
        return result

    def send_back(reduction):
        for step in range(1, owners):
            span = pl.ds(owner_to(step) * tokens, tokens)
            reduction.put(step, slice(0, MODEL_WIDTH), r.total[span].astype(BF16))
            reduction.put(step, slice(MODEL_WIDTH, PACKED), two_parts(r.gate_total[span]))
        reduction.start(0)

    def came_back(reduction):
        back = r.kept_total[...]
        for step in range(1, owners):
            back = back + reduction.coming[step - 1, :, :MODEL_WIDTH].astype(F32)
        terms = reduction.coming[0, :, MODEL_WIDTH:].astype(F32)
        for step in range(2, owners):
            terms = terms + reduction.coming[step - 1, :, MODEL_WIDTH:].astype(F32)
        return back, r.kept_gate[...] + terms + pltpu.roll(terms, LANES - EXPERTS, 1)

    both_cuts = ((0, half), (half, half))
    spread_x0 = Spread(r.packed.at[0], r.plane0, 0)
    spread_x1 = Spread(r.packed.at[1], r.plane1, 1)
    spread_u1 = Spread(r.up, r.ups1, 2)
    spread_u0 = Spread(r.up0, r.ups0, 3)
    mix0 = Reduce(r.leave_y, r.come_y, 0, both_cuts)
    mix1 = Reduce(r.leave_y, r.come_y, 1, both_cuts)
    back1 = Reduce(r.leave_b, r.come_b, 2, ((0, PACKED),))
    back0 = Reduce(r.leave_b, r.come_b, 3, ((0, PACKED),))
    gather_x0 = Gather(0, r.packed.at[0], r.plane0, r.every_x, 0)
    gather_x1 = Gather(1, r.packed.at[1], r.plane1, r.every_x, 1)
    gather_u0 = Gather(0, r.up0, r.ups0, r.every_u, 2)
    gather_u1 = Gather(1, r.up, r.ups1, r.every_u, 3)
    small = [
        SmallGather(layer, source.at[layer], target, 2 * layer + which)
        for layer in range(2)
        for which, (source, target) in enumerate(
            ((r.grad_logits, r.every_logits), (r.gain_grads, r.every_gain))
        )
    ]

    weights_start(0, 0)
    weights_start(0, 1)
    for expert in range(local):
        for copy in swap_pair(expert):
            copy.start()

    @pl.when(section == 0)
    def _():
        for expert in range(local):
            load_in(0, expert)[0].start()
            load_out(0, expert)[0].start()

    r.gain_grads[...] = jnp.zeros_like(r.gain_grads)
    weights_spread(0, 0)
    weights_spread(0, 1)
    weights_push(0, 0)

    def early0():
        weights_start(1, 0)
        weights_start(1, 1)

    def late0():
        weights_push(0, 1)

    attention_forward(0, r.x, early0, late0)
    spread_x0.start()
    spread_u1.start()
    weights_spread(1, 0)
    weights_spread(1, 1)
    spread_x0.wait()
    gather_x0.start()
    gather_x0.start_home()

    def forward_expert(expert, carry):
        @pl.when(section != 0)
        def _():
            for which, make in enumerate((load_in, load_out)):
                swap_pair(expert)[which].wait_recv()
                make(0, expert)[1].start()

        wait_in(expert)

        def work(span, group):
            gate = gate_of(r.plane0, group, expert)
            pair = dot_nn(flat(r.plane0, group, model), r.ein[expert])
            r.pairs[expert, span] = pair.astype(BF16)
            gate_part, up_part = pair[:, :FF], pair[:, FF:]
            silu = gate_part / (1.0 + jnp.exp(-gate_part))
            r.activated[span, expert_columns(expert)] = (silu * up_part * gate).astype(BF16)

        each_chunk(work)
        start_load(load_in, 1, expert, 0, True)
        wait_out(expert)
        return carry

    lax.fori_loop(0, local, forward_expert, 0)
    mix(mix0)
    weights_push(1, 0)
    for expert in range(local):
        start_load(load_out, 1, expert, 1, True)
    gather_u1.start()
    spread_u1.wait()
    gather_u1.start_home()
    mix0.wait()
    r.hidden0[...] = (r.middle[0] + mixed(mix0, r.total[here])).astype(BF16)
    place(0, r.hidden0, r.hidden, 0)

    def late1():
        weights_push(1, 1)

    attention_forward(1, r.hidden0, lambda: None, late1)
    spread_x1.start()
    gather_x0.middle()

    def inner_expert(expert, carry):
        wait_out(expert)

        def work(span, group):
            r.inner[span, expert_columns(expert)] = dot_nt(
                flat(r.ups1, group, model), r.eout[expert_columns(expert)]
            ).astype(r.inner.dtype)

        each_chunk(work)
        return carry

    lax.fori_loop(0, local, inner_expert, 0)
    spread_x1.wait()
    gather_x1.start()
    gather_x1.start_home()
    r.gate_total[...] = jnp.zeros_like(r.gate_total)

    def both_expert(expert, carry):
        wait_in(expert)

        def work(span, group):
            gate = gate_of(r.plane1, group, expert)
            pair = dot_nn(flat(r.plane1, group, model), r.ein[expert])
            inner = r.inner[span, expert_columns(expert)].astype(F32)
            activated = backward_terms(expert, span, gate, pair[:, :FF], pair[:, FF:], inner)
            r.activated[span, expert_columns(expert)] = (activated * gate).astype(BF16)

        each_chunk(work)
        start_load(load_in, 0, expert, 0, False)
        return carry

    lax.fori_loop(0, local, both_expert, 0)
    send_back(back1)
    r.kept_total[...] = r.total[here]
    r.kept_gate[...] = r.gate_total[here]
    gather_u1.middle()
    mix(mix1)
    for expert in range(local):
        start_load(load_out, 0, expert, 1, False)
    back1.wait()
    back, gate_grads = came_back(back1)
    r.up0[...] = attention_backward(1, r.hidden0, r.up, back, gate_grads)
    spread_u0.start()
    place(1, r.up0, r.input_grad, 1)
    small[2].start()
    small[3].start()
    gather_x1.middle()
    mix1.wait()
    r.hidden1[...] = (r.middle[1] + mixed(mix1, r.total[here])).astype(BF16)
    place(1, r.hidden1, r.hidden, 2)
    r.gate_total[...] = jnp.zeros_like(r.gate_total)
    spread_u0.wait()
    gather_u0.start()
    gather_u0.start_home()
    small[2].middle()
    small[3].middle()

    def behind_expert(expert, carry):
        wait_in(expert)
        wait_out(expert)

        def work(span, group):
            gate = gate_of(r.plane0, group, expert)
            pair = r.pairs[expert, span].astype(F32)
            inner = dot_nt(flat(r.ups0, group, model), r.eout[expert_columns(expert)])
            backward_terms(expert, span, gate, pair[:, :FF], pair[:, FF:], inner)

        each_chunk(work)
        return carry

    lax.fori_loop(0, local, behind_expert, 0)
    send_back(back0)
    r.kept_total[...] = r.total[here]
    r.kept_gate[...] = r.gate_total[here]
    gather_u0.middle()
    back0.wait()
    back, gate_grads = came_back(back0)
    r.grad0[...] = attention_backward(0, r.x, r.up0, back, gate_grads)
    place(0, r.grad0, r.input_grad, 3)
    small[0].start()
    small[1].start()
    small[0].middle()
    small[1].middle()

    for layer in range(2):
        for which in range(2):
            weights_unsent(layer, which)
    for expert in range(local):
        for copy in swap_pair(expert):
            copy.wait_send()
    for copy in unsent:
        copy.wait_send()
    for gather in small:
        gather.finish()
    r.gain_sum[...] = jnp.sum(r.every_gain[...].reshape(-1, 8, MODEL_WIDTH), axis=0)
    placed(0, r.hidden0, r.hidden, 0)
    placed(1, r.up0, r.input_grad, 1)
    placed(1, r.hidden1, r.hidden, 2)
    placed(0, r.grad0, r.input_grad, 3)
    for gather in (gather_x0, gather_u1, gather_x1, gather_u0):
        gather.finish()


def both_layers(x, up, attn_in, attn_out, gains, routers, hot, cosine, sine, experts_in, experts_out):
    planes, owners = lax.axis_size("dp"), lax.axis_size("expert")
    tokens = x.shape[0]
    local = experts_in.shape[1]
    slab = attn_in.shape[1]
    rows = owners * tokens
    dma = lambda *shape: pltpu.SemaphoreType.DMA(shape)
    vmem = lambda shape, dtype: pltpu.VMEM(shape, dtype)
    wide = (2, tokens, MODEL_WIDTH)
    everywhere = (owners, planes, 2, tokens)
    inputs = {
        "x": (x, vmem_spec()),
        "up": (up, vmem_spec()),
        "attn_in": (attn_in, any_spec()),
        "attn_out": (attn_out, any_spec()),
        "gains": (gains, vmem_spec()),
        "router": (routers, vmem_spec()),
        "hot": (hot, vmem_spec()),
        "cosine": (cosine, vmem_spec()),
        "sine": (sine, vmem_spec()),
        "experts_in": (experts_in, any_spec()),
        "experts_out": (experts_out, any_spec()),
    }
    outputs = {
        "hidden": (wide, BF16, any_spec()),
        "input_grad": (wide, BF16, any_spec()),
        "other_in": (experts_in.shape[1:], BF16, any_spec()),
        "other_out": (experts_out.shape[1:], BF16, any_spec()),
        "every_x": (everywhere + (PACKED,), BF16, any_spec()),
        "every_u": (everywhere + (MODEL_WIDTH,), BF16, any_spec()),
        "every_logits": (everywhere + (LANES,), BF16, any_spec()),
        "factors": ((2, tokens, PROJECTED + 3 * MODEL_WIDTH), BF16, vmem_spec()),
        "gain_sum": ((8, MODEL_WIDTH), F32, vmem_spec()),
    }
    scratch = {
        "win": vmem((2, MODEL_WIDTH, PROJECTED), BF16),
        "wout": vmem((2, QUERY_WIDTH, MODEL_WIDTH), BF16),
        "ein": vmem((local, MODEL_WIDTH, 2 * FF), BF16),
        "eout": vmem((local * FF, MODEL_WIDTH), BF16),
        "projected": vmem((tokens, PROJECTED), F32),
        "query": vmem(wide, BF16),
        "key": vmem(wide, BF16),
        "value": vmem(wide, BF16),
        "attended": vmem(wide, BF16),
        "logs": vmem((2, 2 * tokens, LANES), F32),
        "middle": vmem(wide, F32),
        "packed": vmem((2, tokens, PACKED), BF16),
        "gates": vmem((2, tokens, LANES), F32),
        "grad_logits": vmem((2, tokens, LANES), BF16),
        "gain_grads": vmem((2, 8, MODEL_WIDTH), F32),
        "every_gain": vmem((owners, planes, 2, 8, MODEL_WIDTH), F32),
        "up0": vmem(wide[1:], BF16),
        "hidden0": vmem(wide[1:], BF16),
        "hidden1": vmem(wide[1:], BF16),
        "grad0": vmem(wide[1:], BF16),
        "grad_middle": vmem(wide[1:], F32),
        "grad_attended": vmem(wide[1:], BF16),
        "plane0": vmem((owners, tokens, PACKED), BF16),
        "plane1": vmem((owners, tokens, PACKED), BF16),
        "ups0": vmem((owners, tokens, MODEL_WIDTH), BF16),
        "ups1": vmem((owners, tokens, MODEL_WIDTH), BF16),
        "pairs": vmem((local, rows, 2 * FF), BF16),
        "inner": vmem((rows, local * FF), BF16),
        "activated": vmem((rows, local * FF), BF16),
        "total": vmem((rows, MODEL_WIDTH), F32),
        "gate_total": vmem((rows, LANES), F32),
        "kept_total": vmem((tokens, MODEL_WIDTH), F32),
        "kept_gate": vmem((tokens, LANES), F32),
        "leave_y": vmem((owners - 1, tokens, MODEL_WIDTH), BF16),
        "come_y": vmem((owners - 1, tokens, MODEL_WIDTH), BF16),
        "leave_b": vmem((owners - 1, tokens, PACKED), BF16),
        "come_b": vmem((owners - 1, tokens, PACKED), BF16),
        "w_local": dma(2, 2),
        "wz_send": dma(2, 2, planes),
        "wz_recv": dma(2, 2, planes),
        "wp_send": dma(2, 2, planes, owners),
        "wp_recv": dma(2, 2, planes, owners),
        "wc_send": dma(2, 2, planes),
        "wc_recv": dma(2, 2, planes),
        "s_send": dma(2, local),
        "s_recv": dma(2, local),
        "l_sem": dma(2, local),
        "a_send": dma(4, owners),
        "a_recv": dma(4, owners),
        "r_send": dma(4, 2, owners),
        "r_recv": dma(4, 2, owners),
        "g_send": dma(4, planes),
        "g_recv": dma(4, planes, 2),
        "g_local": dma(4),
        "gp_send": dma(4, owners),
        "gp_recv": dma(4, owners),
        "q_send": dma(4, planes),
        "q_recv": dma(4, planes, 2),
        "q_local": dma(4),
        "qp_send": dma(4, owners),
        "qp_recv": dma(4, owners),
        "o_send": dma(4),
        "o_recv": dma(4),
        "o_local": dma(4),
    }
    return call(
        functools.partial(layers_kernel, planes, owners, tokens, local, slab),
        "both_layers", 0, inputs, outputs, scratch,
    )


def weight_grad_kernel(
    x_ref, up_ref, gate_ref, win_ref, wout_ref, grad_in_ref, grad_out_ref, activated_ref
):
    expert, block = pl.program_id(0), pl.program_id(1)
    plane = lax.axis_index("dp")
    local = pl.num_programs(0)
    mine = lax.axis_index("expert") * local + expert
    slice_in, slice_out = grad_in_ref.shape[0], grad_out_ref.shape[0]
    lane = lane_of(gate_ref.shape)
    gate = column_of(gate_ref[...], lane, mine)
    pair = dot_nn(x_ref[...], win_ref[...])
    gate_part, up_part = pair[:, :FF], pair[:, FF:]
    sigmoid = 1.0 / (1.0 + jnp.exp(-gate_part))
    silu = gate_part * sigmoid
    activated_ref[...] = (silu * up_part * gate).astype(BF16)
    grad_activated = dot_nt(up_ref[...], wout_ref[...]) * gate
    grad_gate = grad_activated * up_part * sigmoid * (1.0 + gate_part * (1.0 - sigmoid))
    grad_up = grad_activated * silu
    grad_pair = jnp.concatenate([grad_gate.astype(BF16), grad_up.astype(BF16)], axis=-1)
    mine_in = x_ref[:, pl.ds(pl.multiple_of(plane * slice_in, LANES), slice_in)]
    mine_out = activated_ref[:, pl.ds(pl.multiple_of(plane * slice_out, LANES), slice_out)]
    term_in = dot_tn(mine_in, grad_pair)
    term_out = dot_tn(mine_out, up_ref[...])

    @pl.when(block == 0)
    def _():
        grad_in_ref[...] = term_in
        grad_out_ref[...] = term_out

    @pl.when(block > 0)
    def _():
        grad_in_ref[...] += term_in
        grad_out_ref[...] += term_out


def weight_grads(x, up, experts_in, experts_out):
    planes = lax.axis_size("dp")
    local = experts_in.shape[1]
    rows = x.shape[0]
    block = 512
    shape = jax.ShapeDtypeStruct
    return pl.pallas_call(
        weight_grad_kernel,
        grid=(local, rows // block),
        out_shape=(
            shape((local, MODEL_WIDTH // planes, 2 * FF), F32),
            shape((local, FF // planes, MODEL_WIDTH), F32),
        ),
        in_specs=[
            pl.BlockSpec((block, MODEL_WIDTH), lambda e, b: (b, 0)),
            pl.BlockSpec((block, MODEL_WIDTH), lambda e, b: (b, 0)),
            pl.BlockSpec((block, LANES), lambda e, b: (b, MODEL_WIDTH // LANES)),
            pl.BlockSpec((None, None, MODEL_WIDTH, 2 * FF), lambda e, b: (0, e, 0, 0)),
            pl.BlockSpec((None, None, FF, MODEL_WIDTH), lambda e, b: (0, e, 0, 0)),
        ],
        out_specs=(
            pl.BlockSpec((None, MODEL_WIDTH // planes, 2 * FF), lambda e, b: (e, 0, 0)),
            pl.BlockSpec((None, FF // planes, MODEL_WIDTH), lambda e, b: (e, 0, 0)),
        ),
        scratch_shapes=[pltpu.VMEM((block, FF), BF16)],
        compiler_params=pltpu.CompilerParams(vmem_limit_bytes=VMEM_LIMIT),
        name="weight_grads",
    )(x, up, x, experts_in, experts_out)


def rotated_blocks(block, axis):
    length = lax.axis_size(axis)
    blocks = [block]
    for step in range(1, length):
        blocks.append(lax.ppermute(block, axis, [(i, (i + step) % length) for i in range(length)]))
    return jnp.stack(blocks)


def shards(layer_input, cotangent, positions, routes, gain_one, attn_in, attn_out, gain_two, router,
           experts_in, experts_out):
    section = lax.axis_index("section")
    first = section == 0
    planes = lax.axis_size("dp")
    owners = lax.axis_size("expert")
    own = lax.axis_index("expert")
    tokens = layer_input.shape[1]

    def swap(values):
        return lax.ppermute(values, "section", [(0, 1), (1, 0)])

    def layered(mine, other):
        return jnp.stack([jnp.where(first, mine, other), jnp.where(first, other, mine)])

    def both(mine):
        return layered(mine, swap(mine))

    gains = both(jnp.concatenate([gain_one, gain_two], axis=0))
    routers = both(jnp.pad(router[0], ((0, 0), (0, LANES - EXPERTS))))

    pick = functools.partial(lax.dynamic_index_in_dim, axis=0, keepdims=False)
    x = pick(layer_input, section)
    up = pick(cotangent, section)
    place = pick(positions, section)
    choices = layered(pick(routes[0], section), swap(pick(routes[0], 1 - section)))
    hot = jnp.sum(
        (choices[..., None] == jnp.arange(LANES, dtype=jnp.int32)).astype(F32), axis=2
    )
    lane = jnp.arange(LANES)
    frequency = jnp.power(rotary_base, -((lane % HALF).astype(F32) * (2.0 / HEAD_SIZE)))
    angles = place.astype(F32)[:, None] * frequency[None, :]
    cosine = jnp.cos(angles)
    sine = jnp.where(lane % HEAD_SIZE < HALF, -1.0, 1.0) * jnp.sin(angles)

    done = both_layers(
        x, up, attn_in, attn_out, gains, routers, hot, cosine, sine, experts_in, experts_out
    )
    every_x = done["every_x"].reshape(-1, PACKED)
    every_u = done["every_u"].reshape(-1, MODEL_WIDTH)
    every_logits = done["every_logits"].reshape(-1, LANES)
    grad_experts_in, grad_experts_out = weight_grads(every_x, every_u, experts_in, experts_out)
    grad_router = dot_tn(every_x[:, :MODEL_WIDTH], every_logits)[:, :EXPERTS]

    factors = jnp.concatenate(
        [pick(done["factors"], section), swap(pick(done["factors"], 1 - section))], axis=0
    )
    around = rotated_blocks(factors, "expert").reshape(-1, factors.shape[1])
    part = MODEL_WIDTH // (planes * owners)

    def mine_of(values):
        blocks = values.reshape(-1, planes, owners, part)
        return lax.dynamic_index_in_dim(blocks, own, 2, keepdims=False).reshape(-1, planes * part)

    start = PROJECTED + MODEL_WIDTH
    grad_in = dot_tn(mine_of(around[:, start : start + MODEL_WIDTH]), around[:, :PROJECTED])
    grad_out = dot_tn(mine_of(around[:, start + MODEL_WIDTH :]), around[:, PROJECTED:start])
    partial = jnp.concatenate([grad_in, grad_out], axis=-1).reshape(planes, part, -1)
    plane = lax.axis_index("dp")
    total = pick(partial, plane)
    for step in range(1, planes):
        leaving = pick(partial, (plane + step) % planes).astype(BF16)
        pairs = [(i, (i + step) % planes) for i in range(planes)]
        total = total + lax.ppermute(leaving, "dp", pairs).astype(F32)
    grad_attn_in, grad_attn_out = total[:, :PROJECTED], total[:, PROJECTED:]

    return (
        done["hidden"][None],
        done["input_grad"][None],
        done["gain_sum"][0:1],
        grad_attn_in[None],
        grad_attn_out[None],
        done["gain_sum"][1:2],
        grad_router[None],
        grad_experts_in[None],
        grad_experts_out[None],
    )


def solution(mesh):
    in_specs = (
        P(None, ("dp", "expert"), None),
        P(None, ("dp", "expert"), None),
        P(None, ("dp", "expert")),
        P("section", None, ("dp", "expert"), None),
        P("section", None),
        P("section", "dp", None),
        P("section", "dp", None),
        P("section", None),
        P("section", None, None),
        P("section", "expert", None, None),
        P("section", "expert", None, None),
    )
    out_specs = (
        P("section", None, ("dp", "expert"), None),
        P("section", None, ("dp", "expert"), None),
        P("section", None),
        P("section", ("dp", "expert"), None),
        P("section", ("dp", "expert"), None),
        P("section", None),
        P("section", None, None),
        P("section", "expert", "dp", None),
        P("section", "expert", "dp", None),
    )
    return jax.shard_map(shards, mesh=mesh, in_specs=in_specs, out_specs=out_specs, check_vma=False)
```

time: 576 us -> 427 us (0.74)
  blocking collectives: 74.1 us -> 0 us
  waiting for transfers between devices: 91.8 us -> 58.7 us
  local copies, waits for them, and re-layouts: 30.9 us -> 16.5 us
  other arithmetic: 24.7 us -> 12.1 us
  starting transfers between devices: 15.5 us -> 9.3 us
  Pallas kernels: 327 us -> 321 us
    psum x1 -> x0, blocking collectives: 74.1 us -> none  [shards(): gain_sums = lax.psum(gain_mine + gain_other, ('dp', 'expert'))]
    ppermute x3, waiting for transfers between devices: 27.5 us -> 0.01 us  [shards(): total = total + lax.ppermute(leaving, 'dp', pairs).astype(F32)]
    another operation x5 -> x2, other arithmetic: 13.5 us -> 4.23 us  [rotated_blocks(): return jnp.stack(blocks)]
    unnamed x72 -> x13, local copies, waits for them, and re-layouts: 17.3 us -> 8.27 us
    ppermute x9 -> x3, starting transfers between devices: 13.1 us -> 4.24 us  [rotated_blocks(): lax.ppermute(block, axis, [(i, (i + step) % length) for i in range(length)])]
    pallas_call x8 -> x1, Pallas kernels: 236 us -> 229 us  [call(): pl.pallas_call(body, out_shape=tuple((jax.ShapeDtypeStruct(shape, dtype)...]
    ppermute x9 -> x3, waiting for transfers between devices: 61.7 us -> 56.6 us  [rotated_blocks(): lax.ppermute(block, axis, [(i, (i + step) % length) for i in range(length)])]
  transfers between devices with their start and end apart: 22 -> 10, of which waited for: 10 -> 3; matrix products, arithmetic and copies ran while one was open for 7% -> 3% of each run, Pallas kernels for 17% -> 22%
where the time goes in v2:
time: 427 us; the launch traced here: 426 us
  Pallas kernels  321 us (75%)
  waiting for transfers between devices  58.7 us (14%)
  local copies, waits for them, and re-layouts  16.5 us (4%)
  other arithmetic  12.1 us (3%)
  starting transfers between devices  9.3 us (2%)
  matrix products  7.79 us (2%)
    pallas_call x1, Pallas kernels, call(): pl.pallas_call(body, out_shape=tuple((jax.ShapeDtypeStruct(shape, dtype)...  229 us
    pallas_call x1, Pallas kernels, weight_grads(): pl.pallas_call(weight_grad_kernel, grid=(local, rows // block), out_shape...  91.7 us
    ppermute x3, waiting for transfers between devices, rotated_blocks(): lax.ppermute(block, axis, [(i, (i + step) % length) for i in range(length)])  56.6 us
  transfers between devices with their start and end apart: 10, of which 3 were waited for; matrix products, arithmetic and copies ran while one was open for 3% of the time, Pallas kernels for 22%

profile of v2, /device:TPU:0, one launch (start us, length us, event | category | flops | bytes accessed | tf_op | source)
XLA Modules:
  0.0 426.3 jit_solution(4883305295597805264)
XLA Ops:
  0.6 0.7 dynamic-slice_bitcast_fusion.4
  1.8 1.0 copy.30
  3.0 0.7 pad_maximum_fusion.5
  4.9 0.8 fusion.15
  5.8 1.7 dynamic-slice_bitcast_fusion.2
  8.2 0.9 convert_reduce_fusion.refs_6_
  9.1 0.7 select_bitcast_fusion.3
  10.6 0.8 pad_maximum_fusion.3.refs_5_
  11.4 229.4 %both_layers.1 = (bf16[2,64,1024]{2,1,0:T(8,128)(2,1)}, bf16[2,64,1024]{2,1,0:T(8,128)(2,1)}, bf16[8,1024,1024]{2,1,0:T(8,128)(2,1)}, bf16[8,512,1024]{2,1,0:T(8...) custom-call(bf16[64,1024]{1,0:T(8,128)(2,1)} %get-tuple-element.49.r, ...), custom_call_target="tpu_custom_call" | custom-call | tf_op jit(solution)/shard_map/both_layers/pallas_call | solution.py:101
  240.8 1.4 dynamic-slice_bitcast_fusion.1
  242.2 2.1 collective-permute-done.3
  244.3 1.4 fusion.24
  246.3 3.3 collective-permute-start.5
  249.9 28.9 %collective-permute-done.4 = bf16[128,5120]{1,0:T(8,128)(2,1)S(1)} collective-permute-done((bf16[128,5120]{1,0:T(8,128)(2,1)}, bf16[128,5120]{1,0:T(8,128)(2,1)S(1)}, u32[]{:S(2)}, u32[]{:S(2)}) %collective-permute-start.4) | collective-permute-done | bytes 1310752 | tf_op jit(solution)/shard_map/ppermute | solution.py:1032
  278.9 27.7 %collective-permute-done.5 = bf16[128,5120]{1,0:T(8,128)(2,1)} collective-permute-done((bf16[128,5120]{1,0:T(8,128)(2,1)}, bf16[128,5120]{1,0:T(8,128)(2,1)}, u32[]{:S(2)}, u32[]{:S(2)}) %collective-permute-start.5) | collective-permute-done | bytes 1310752 | tf_op jit(solution)/shard_map/ppermute | solution.py:1032
  306.5 2.9 pad_maximum_fusion
  309.4 2.3 copy-done
  312.5 2.3 fusion.2
  314.9 1.3 copy.35
  316.2 1.0 constant_dynamic-slice_fusion
  317.2 1.7 fusion.7
  319.2 1.6 copy-done.1
  321.0 0.8 collective-permute-start.7
  322.0 2.8 collective-permute-start.9
  324.9 1.4 fusion.26
  326.3 91.7 %weight_grads.1 = (f32[8,256,1024]{2,1,0:T(8,128)}, f32[8,128,1024]{2,1,0:T(8,128)}) custom-call(bf16[2048,1152]{1,0:T(8,128)(2,1)} %bitcast.73, bf16[2048,1024]{1,0:T(8,128)(2,1)} %bitcast.78, bf16[2048,1152]{1,0:T(8,128)(2,1)} %bitcast.74, bf16[1,8,1024,1024]{3,2,1,0:T(8,128)(2,1)} %win_ref.1, bf16[1,8,512,1024]{3,2,1,0:T(8,128)(2,1)} %wout_ref.1), custom_call_target="tpu_custom_call" | custom-call | tf_op jit(solution)/shard_map/weight_grads/pallas_call | solution.py:1004
  418.0 3.8 fusion.4
  421.8 1.5 fusion.10
  423.3 0.8 slice_bitcast_fusion
  424.1 0.7 slice_bitcast_fusion.1
  424.9 0.7 copy.38
  425.6 0.7 copy.39
  (33 shorter events, 5.9 us)
Async XLA Ops:
  1.3 6.1 %collective-permute-start.2 = (s32[64,8]{0,1:T(8,128)S(1)}, s32[64,8]{0,1:T(8,128)S(1)}, u32[]{:S(2)}, u32[]{:S(2)}) collective-permute-start(s32[64,8]{0,1:T(8,128)S(1)} %dynamic-slice_bitcast_fusion.4), channel_id=1, source_target_pairs={{0,16},{16,0},{1,17},{17,1},{2,18},{18,2},{3,19},{19,3},{4,20},{20... | collective-permute-start | bytes 6152 | tf_op jit(solution)/shard_map/ppermute | solution.py:1046
  2.9 7.6 %collective-permute-start.1 = (bf16[1024,128]{1,0:T(8,128)(2,1)S(1)}, bf16[1024,128]{1,0:T(8,128)(2,1)S(1)}, u32[]{:S(2)}, u32[]{:S(2)}) collective-permute-start(bf16[1024,128]{1,0:T(8,128)(2,1)S(1)} %pad.4), channel_id=1, source_target_pairs={{0,16},{16,0},{1,17},{17,1},{2,18},{18,2},{3,19},{19,3},{4,20},{20... | collective-permute-start | bytes 786440 | tf_op jit(solution)/shard_map/ppermute | solution.py:1046
  3.7 5.4 %collective-permute-start = (f32[2,1024]{1,0:T(2,128)S(1)}, f32[2,1024]{1,0:T(2,128)S(1)}, u32[]{:S(2)}, u32[]{:S(2)}) collective-permute-start(f32[2,1024]{1,0:T(2,128)S(1)} %pad_maximum_fusion.5), channel_id=1, source_target_pairs={{0,16},{16,0},{1,17},{17,1},{2,18},{18,2},{3,19},{19,3},{4,20},{20... | collective-permute-start | bytes 24584 | tf_op jit(solution)/shard_map/ppermute | solution.py:1046
  242.2 2.2 collective-permute-start.3
  245.7 33.2 %collective-permute-start.4 = (bf16[128,5120]{1,0:T(8,128)(2,1)}, bf16[128,5120]{1,0:T(8,128)(2,1)S(1)}, u32[]{:S(2)}, u32[]{:S(2)}) collective-permute-start(bf16[128,5120]{1,0:T(8,128)(2,1)} %get-tuple-element.33), channel_id=1, source_target_pairs={{0,1},{1,2},{2,3},{3,0},{4,5},{5,6},{6,7},{7,4},{8,9},{9,10},{10,1... | collective-permute-start | bytes 3932168 | tf_op jit(solution)/shard_map/ppermute | solution.py:1032
  246.3 60.3 %collective-permute-start.5 = (bf16[128,5120]{1,0:T(8,128)(2,1)}, bf16[128,5120]{1,0:T(8,128)(2,1)}, u32[]{:S(2)}, u32[]{:S(2)}) collective-permute-start(bf16[128,5120]{1,0:T(8,128)(2,1)} %get-tuple-element.33), channel_id=1, source_target_pairs={{0,2},{1,3},{2,0},{3,1},{4,6},{5,7},{6,4},{7,5},{8,10},{9,11},{10,... | collective-permute-start | bytes 3932168 | tf_op jit(solution)/shard_map/ppermute | solution.py:1032
  249.6 56.9 %collective-permute-start.6 = (bf16[128,5120]{1,0:T(8,128)(2,1)}, bf16[128,5120]{1,0:T(8,128)(2,1)}, u32[]{:S(2)}, u32[]{:S(2)}) collective-permute-start(bf16[128,5120]{1,0:T(8,128)(2,1)} %get-tuple-element.33), channel_id=1, source_target_pairs={{0,3},{1,0},{2,1},{3,2},{4,7},{5,4},{6,5},{7,6},{8,11},{9,8},{10,9... | collective-permute-start | bytes 3932168 | tf_op jit(solution)/shard_map/ppermute | solution.py:1032
  309.4 2.4 copy-start
  319.2 1.6 copy-start.1
  321.0 100.8 %collective-permute-start.7 = (bf16[64,3072]{1,0:T(8,128)(2,1)S(1)}, bf16[64,3072]{1,0:T(8,128)(2,1)S(1)}, u32[]{:S(2)}, u32[]{:S(2)}) collective-permute-start(bf16[64,3072]{1,0:T(8,128)(2,1)S(1)} %get-tuple-element.29), channel_id=1, source_target_pairs={{0,4},{4,8},{8,12},{12,0},{1,5},{5,9},{9,13},{13,1},{2,6},{6,10},{... | collective-permute-start | bytes 1179656 | tf_op jit(solution)/shard_map/ppermute | solution.py:1099
  321.8 100.0 %collective-permute-start.8 = (bf16[64,3072]{1,0:T(8,128)(2,1)S(1)}, bf16[64,3072]{1,0:T(8,128)(2,1)S(1)}, u32[]{:S(2)}, u32[]{:S(2)}) collective-permute-start(bf16[64,3072]{1,0:T(8,128)(2,1)S(1)} %get-tuple-element.31), channel_id=1, source_target_pairs={{0,8},{4,12},{8,0},{12,4},{1,9},{5,13},{9,1},{13,5},{2,10},{6,14},... | collective-permute-start | bytes 1179656 | tf_op jit(solution)/shard_map/ppermute | solution.py:1099
  322.0 99.8 %collective-permute-start.9 = (bf16[64,3072]{1,0:T(8,128)(2,1)S(1)}, bf16[64,3072]{1,0:T(8,128)(2,1)}, u32[]{:S(2)}, u32[]{:S(2)}) collective-permute-start(bf16[64,3072]{1,0:T(8,128)(2,1)S(1)} %get-tuple-element.30), channel_id=1, source_target_pairs={{0,12},{4,0},{8,4},{12,8},{1,13},{5,1},{9,5},{13,9},{2,14},{6,2},{... | collective-permute-start | bytes 1179656 | tf_op jit(solution)/shard_map/ppermute | solution.py:1099
  421.8 3.1 copy-start.3
  421.8 3.8 copy-start.2

commit v3 on v2

--- a/solution.py
+++ b/solution.py
@@ -960,12 +960,10 @@
     )
 
 
-def weight_grad_kernel(
-    x_ref, up_ref, gate_ref, win_ref, wout_ref, grad_in_ref, grad_out_ref, activated_ref
-):
-    expert, block = pl.program_id(0), pl.program_id(1)
+def weight_grad_kernel(start, local, x_ref, up_ref, gate_ref, win_ref, wout_ref, *refs):
+    grad_in_ref, grad_out_ref, activated_ref = refs[-3:]
+    expert, block = start + pl.program_id(0), pl.program_id(1)
     plane = lax.axis_index("dp")
-    local = pl.num_programs(0)
     mine = lax.axis_index("expert") * local + expert
     slice_in, slice_out = grad_in_ref.shape[0], grad_out_ref.shape[0]
     lane = lane_of(gate_ref.shape)
@@ -995,42 +993,37 @@
         grad_out_ref[...] += term_out
 
 
-def weight_grads(x, up, experts_in, experts_out):
+def weight_grads(x, up, experts_in, experts_out, start, count, before):
     planes = lax.axis_size("dp")
     local = experts_in.shape[1]
     rows = x.shape[0]
     block = 512
     shape = jax.ShapeDtypeStruct
+    slice_in, slice_out = MODEL_WIDTH // planes, FF // planes
+    multiplies = rows * count * (3 * MODEL_WIDTH * FF + 2 * FF * slice_in + MODEL_WIDTH * slice_out)
     return pl.pallas_call(
-        weight_grad_kernel,
-        grid=(local, rows // block),
-        out_shape=(
-            shape((local, MODEL_WIDTH // planes, 2 * FF), F32),
-            shape((local, FF // planes, MODEL_WIDTH), F32),
-        ),
+        functools.partial(weight_grad_kernel, start, local),
+        grid=(count, rows // block),
+        out_shape=(shape((local, slice_in, 2 * FF), F32), shape((local, slice_out, MODEL_WIDTH), F32)),
         in_specs=[
             pl.BlockSpec((block, MODEL_WIDTH), lambda e, b: (b, 0)),
             pl.BlockSpec((block, MODEL_WIDTH), lambda e, b: (b, 0)),
             pl.BlockSpec((block, LANES), lambda e, b: (b, MODEL_WIDTH // LANES)),
-            pl.BlockSpec((None, None, MODEL_WIDTH, 2 * FF), lambda e, b: (0, e, 0, 0)),
-            pl.BlockSpec((None, None, FF, MODEL_WIDTH), lambda e, b: (0, e, 0, 0)),
-        ],
+            pl.BlockSpec((None, None, MODEL_WIDTH, 2 * FF), lambda e, b: (0, start + e, 0, 0)),
+            pl.BlockSpec((None, None, FF, MODEL_WIDTH), lambda e, b: (0, start + e, 0, 0)),
+        ] + [any_spec()] * len(before),
         out_specs=(
-            pl.BlockSpec((None, MODEL_WIDTH // planes, 2 * FF), lambda e, b: (e, 0, 0)),
-            pl.BlockSpec((None, FF // planes, MODEL_WIDTH), lambda e, b: (e, 0, 0)),
+            pl.BlockSpec((None, slice_in, 2 * FF), lambda e, b: (start + e, 0, 0)),
+            pl.BlockSpec((None, slice_out, MODEL_WIDTH), lambda e, b: (start + e, 0, 0)),
         ),
         scratch_shapes=[pltpu.VMEM((block, FF), BF16)],
+        input_output_aliases={5 + i: i for i in range(len(before))},
         compiler_params=pltpu.CompilerParams(vmem_limit_bytes=VMEM_LIMIT),
+        cost_estimate=pl.CostEstimate(
+            flops=3 * multiplies, bytes_accessed=count * rows * 4 * MODEL_WIDTH, transcendentals=0
+        ),
         name="weight_grads",
-    )(x, up, x, experts_in, experts_out)
-
-
-def rotated_blocks(block, axis):
-    length = lax.axis_size(axis)
-    blocks = [block]
-    for step in range(1, length):
-        blocks.append(lax.ppermute(block, axis, [(i, (i + step) % length) for i in range(length)]))
-    return jnp.stack(blocks)
+    )(x, up, x, experts_in, experts_out, *before)
 
 
 def shards(layer_input, cotangent, positions, routes, gain_one, attn_in, attn_out, gain_two, router,
@@ -1074,13 +1067,18 @@
     every_x = done["every_x"].reshape(-1, PACKED)
     every_u = done["every_u"].reshape(-1, MODEL_WIDTH)
     every_logits = done["every_logits"].reshape(-1, LANES)
-    grad_experts_in, grad_experts_out = weight_grads(every_x, every_u, experts_in, experts_out)
-    grad_router = dot_tn(every_x[:, :MODEL_WIDTH], every_logits)[:, :EXPERTS]
 
     factors = jnp.concatenate(
         [pick(done["factors"], section), swap(pick(done["factors"], 1 - section))], axis=0
     )
-    around = rotated_blocks(factors, "expert").reshape(-1, factors.shape[1])
+    blocks = [factors]
+    for step in range(1, owners):
+        pairs = [(i, (i + step) % owners) for i in range(owners)]
+        blocks.append(lax.ppermute(factors, "expert", pairs))
+    local = experts_in.shape[1]
+    early = weight_grads(every_x, every_u, experts_in, experts_out, 0, local // 2, ())
+    blocks, early = lax.optimization_barrier((blocks, early))
+    around = jnp.concatenate(blocks, axis=0)
     part = MODEL_WIDTH // (planes * owners)
 
     def mine_of(values):
@@ -1093,10 +1091,21 @@
     partial = jnp.concatenate([grad_in, grad_out], axis=-1).reshape(planes, part, -1)
     plane = lax.axis_index("dp")
     total = pick(partial, plane)
+    leaving = [pick(partial, (plane + step) % planes).astype(BF16) for step in range(1, planes)]
+    early, leaving = lax.optimization_barrier((early, leaving))
+    arriving = []
     for step in range(1, planes):
-        leaving = pick(partial, (plane + step) % planes).astype(BF16)
         pairs = [(i, (i + step) % planes) for i in range(planes)]
-        total = total + lax.ppermute(leaving, "dp", pairs).astype(F32)
+        arriving.append(lax.ppermute(leaving[step - 1], "dp", pairs))
+    grad_experts_in, grad_experts_out = weight_grads(
+        every_x, every_u, experts_in, experts_out, local // 2, local - local // 2, early
+    )
+    grad_router = dot_tn(every_x[:, :MODEL_WIDTH], every_logits)[:, :EXPERTS]
+    arriving, grad_experts_in, grad_experts_out, grad_router = lax.optimization_barrier(
+        (arriving, grad_experts_in, grad_experts_out, grad_router)
+    )
+    for piece in arriving:
+        total = total + piece.astype(F32)
     grad_attn_in, grad_attn_out = total[:, :PROJECTED], total[:, PROJECTED:]
 
     return (

time: 427 us -> 378 us (0.89)
  waiting for transfers between devices: 58.7 us -> 7.33 us
    ppermute x6, waiting for transfers between devices: 56.6 us -> 5.28 us  [the longest x3 5.27 us: shards(): blocks.append(lax.ppermute(factors, 'expert', pairs))]
    pallas_call x1 -> x2, Pallas kernels: 91.7 us -> 95.2 us  [weight_grads(): pl.pallas_call(functools.partial(weight_grad_kernel, start, local), grid=...]
    unnamed x13 -> x16, local copies, waits for them, and re-layouts: 8.27 us -> 9.28 us
  transfers between devices with their start and end apart: 10 -> 10, of which waited for: 3 -> 2; matrix products, arithmetic and copies ran while one was open for 3% -> 3% of each run, Pallas kernels for 22% -> 25%
where the time goes in v3:
time: 378 us; the launch traced here: 377 us
  Pallas kernels  325 us (86%)
  local copies, waits for them, and re-layouts  19 us (5%)
  starting transfers between devices  9.39 us (2%)
  other arithmetic  7.98 us (2%)
  matrix products  7.67 us (2%)
  waiting for transfers between devices  7.33 us (2%)
    pallas_call x1, Pallas kernels, call(): pl.pallas_call(body, out_shape=tuple((jax.ShapeDtypeStruct(shape, dtype)...  229 us
    pallas_call x2, Pallas kernels, weight_grads(): pl.pallas_call(functools.partial(weight_grad_kernel, start, local), grid=...  95.2 us
    unnamed x16, local copies, waits for them, and re-layouts  9.28 us
    dot_general x3, matrix products, dot_tn(): lax.dot_general(a, b, (((0,), (0,)), ((), ())), preferred_element_type=F32)  7.67 us
  transfers between devices with their start and end apart: 10, of which 2 were waited for; matrix products, arithmetic and copies ran while one was open for 3% of the time, Pallas kernels for 25%

profile of v3, /device:TPU:0, one launch (start us, length us, event | category | flops | bytes accessed | tf_op | source)
XLA Modules:
  0.0 376.9 jit_solution(11596276509378473302)
XLA Ops:
  0.6 0.7 dynamic-slice_bitcast_fusion.4
  1.8 0.7 pad_maximum_fusion.4
  2.6 1.0 copy.30
  4.9 0.8 fusion.12
  5.8 1.7 dynamic-slice_bitcast_fusion.2
  7.4 0.7 fusion.13
  8.2 0.9 convert_reduce_fusion.refs_6_
  9.1 0.7 select_bitcast_fusion.3
  10.6 0.8 pad_maximum_fusion.2.refs_5_
  11.4 229.4 %both_layers.1 = (bf16[2,64,1024]{2,1,0:T(8,128)(2,1)}, bf16[2,64,1024]{2,1,0:T(8,128)(2,1)}, bf16[8,1024,1024]{2,1,0:T(8,128)(2,1)}, bf16[8,512,1024]{2,1,0:T(8...) custom-call(bf16[64,1024]{1,0:T(8,128)(2,1)} %get-tuple-element.85.r, ...), custom_call_target="tpu_custom_call" | custom-call | tf_op jit(solution)/shard_map/both_layers/pallas_call | solution.py:101
  240.8 1.4 dynamic-slice_bitcast_fusion.1
  242.3 2.0 collective-permute-done.3
  244.4 3.4 collective-permute-start.6
  248.5 47.7 %weight_grads.2 = (f32[8,256,1024]{2,1,0:T(8,128)}, f32[8,128,1024]{2,1,0:T(8,128)}) custom-call(bf16[2048,1152]{1,0:T(8,128)(2,1)} %bitcast.73, bf16[2048,1024]{1,0:T(8,128)(2,1)} %bitcast.78, bf16[2048,1152]{1,0:T(8,128)(2,1)} %bitcast.74, bf16[1,8,1024,1024]{3,2,1,0:T(8,128)(2,1)} %win_ref.3, bf16[1,8,512,1024]{3,2,1,0:T(8,128)(2,1)} %wout_ref.3), custom_call_target="tpu_custom_call" | custom-call | flops 48318382080 | bytes 33554432 | tf_op jit(solution)/shard_map/weight_grads/pallas_call | solution.py:1004
  296.2 1.4 fusion.22
  297.6 3.7 fusion
  301.3 5.3 %collective-permute-done.5 = bf16[128,5120]{1,0:T(8,128)(2,1)} collective-permute-done((bf16[128,5120]{1,0:T(8,128)(2,1)S(1)}, bf16[128,5120]{1,0:T(8,128)(2,1)}, u32[]{:S(2)}, u32[]{:S(2)}) %collective-permute-start.5) | collective-permute-done | bytes 1310752 | tf_op jit(solution)/shard_map/ppermute | solution.py:1077
  306.7 1.4 constant_dynamic-update-slice_fusion.2
  308.1 1.4 constant_dynamic-update-slice_fusion.1
  309.5 1.4 constant_dynamic-update-slice_fusion
  310.9 2.3 copy-done.1
  314.6 1.7 fusion.4
  316.3 2.3 fusion.2
  318.9 1.6 copy-done
  320.7 1.1 collective-permute-start.7
  322.0 2.8 collective-permute-start.9
  324.9 47.5 %weight_grads.3 = (f32[8,256,1024]{2,1,0:T(8,128)}, f32[8,128,1024]{2,1,0:T(8,128)}) custom-call(bf16[2048,1152]{1,0:T(8,128)(2,1)} %bitcast.76, bf16[2048,1024]{1,0:T(8,128)(2,1)} %bitcast.79, bf16[2048,1152]{1,0:T(8,128)(2,1)} %bitcast.77, bf16[1,8,1024,1024]{3,2,1,0:T(8,128)(2,1)} %win_ref.3, ...), custom_call_target="tpu_custom_call", output_to_operand_aliasing={{0}: (5, {}), {1}: (6, {})} | custom-call | flops 48318382080 | bytes 33554432 | tf_op jit(solution)/shard_map/weight_grads/pallas_call | solution.py:1004
  372.4 1.5 fusion.7
  373.9 0.7 slice_bitcast_fusion.1
  374.6 0.8 slice_bitcast_fusion
  375.5 0.7 copy.41
  376.2 0.7 copy.42
  (39 shorter events, 5.6 us)
Async XLA Ops:
  1.3 6.1 %collective-permute-start.2 = (s32[64,8]{0,1:T(8,128)S(1)}, s32[64,8]{0,1:T(8,128)S(1)}, u32[]{:S(2)}, u32[]{:S(2)}) collective-permute-start(s32[64,8]{0,1:T(8,128)S(1)} %dynamic-slice_bitcast_fusion.4), channel_id=1, source_target_pairs={{0,16},{16,0},{1,17},{17,1},{2,18},{18,2},{3,19},{19,3},{4,20},{20... | collective-permute-start | bytes 6152 | tf_op jit(solution)/shard_map/ppermute | solution.py:1039
  2.5 6.6 %collective-permute-start = (f32[2,1024]{1,0:T(2,128)S(1)}, f32[2,1024]{1,0:T(2,128)S(1)}, u32[]{:S(2)}, u32[]{:S(2)}) collective-permute-start(f32[2,1024]{1,0:T(2,128)S(1)} %pad_maximum_fusion.4), channel_id=1, source_target_pairs={{0,16},{16,0},{1,17},{17,1},{2,18},{18,2},{3,19},{19,3},{4,20},{20... | collective-permute-start | bytes 24584 | tf_op jit(solution)/shard_map/ppermute | solution.py:1039
  3.7 6.7 %collective-permute-start.1 = (bf16[1024,128]{1,0:T(8,128)(2,1)S(1)}, bf16[1024,128]{1,0:T(8,128)(2,1)S(1)}, u32[]{:S(2)}, u32[]{:S(2)}) collective-permute-start(bf16[1024,128]{1,0:T(8,128)(2,1)S(1)} %pad.4), channel_id=1, source_target_pairs={{0,16},{16,0},{1,17},{17,1},{2,18},{18,2},{3,19},{19,3},{4,20},{20... | collective-permute-start | bytes 786440 | tf_op jit(solution)/shard_map/ppermute | solution.py:1039
  242.2 2.2 collective-permute-start.3
  244.4 56.9 %collective-permute-start.6 = (bf16[128,5120]{1,0:T(8,128)(2,1)S(1)}, bf16[128,5120]{1,0:T(8,128)(2,1)}, u32[]{:S(2)}, u32[]{:S(2)}) collective-permute-start(bf16[128,5120]{1,0:T(8,128)(2,1)S(1)} %pad_maximum_fusion.1), channel_id=1, source_target_pairs={{0,3},{1,0},{2,1},{3,2},{4,7},{5,4},{6,5},{7,6},{8,11},{9,8},{10,9... | collective-permute-start | bytes 3932168 | tf_op jit(solution)/shard_map/ppermute | solution.py:1077
  247.9 58.7 %collective-permute-start.5 = (bf16[128,5120]{1,0:T(8,128)(2,1)S(1)}, bf16[128,5120]{1,0:T(8,128)(2,1)}, u32[]{:S(2)}, u32[]{:S(2)}) collective-permute-start(bf16[128,5120]{1,0:T(8,128)(2,1)S(1)} %pad_maximum_fusion.1), channel_id=1, source_target_pairs={{0,2},{1,3},{2,0},{3,1},{4,6},{5,7},{6,4},{7,5},{8,10},{9,11},{10,... | collective-permute-start | bytes 3932168 | tf_op jit(solution)/shard_map/ppermute | solution.py:1077
  247.9 58.7 %collective-permute-start.4 = (bf16[128,5120]{1,0:T(8,128)(2,1)S(1)}, bf16[128,5120]{1,0:T(8,128)(2,1)}, u32[]{:S(2)}, u32[]{:S(2)}) collective-permute-start(bf16[128,5120]{1,0:T(8,128)(2,1)S(1)} %pad_maximum_fusion.1), channel_id=1, source_target_pairs={{0,1},{1,2},{2,3},{3,0},{4,5},{5,6},{6,7},{7,4},{8,9},{9,10},{10,1... | collective-permute-start | bytes 3932168 | tf_op jit(solution)/shard_map/ppermute | solution.py:1077
  248.5 49.1 %copy-start.4 = (bf16[4,4,2,64,128]{4,3,2,1,0:T(8,128)(2,1)S(1)}, bf16[4,4,2,64,128]{4,3,2,1,0:T(8,128)(2,1)}, u32[]{:S(2)}) copy-start(bf16[4,4,2,64,128]{4,3,2,1,0:T(8,128)(2,1)} %get-tuple-element.58) | copy-start | bytes 1572868
  310.9 2.3 copy-start.1
  318.9 1.6 copy-start
  320.7 51.7 %collective-permute-start.7 = (bf16[64,3072]{1,0:T(8,128)(2,1)S(1)}, bf16[64,3072]{1,0:T(8,128)(2,1)S(1)}, u32[]{:S(2)}, u32[]{:S(2)}) collective-permute-start(bf16[64,3072]{1,0:T(8,128)(2,1)S(1)} %get-tuple-element.51), channel_id=1, source_target_pairs={{0,4},{4,8},{8,12},{12,0},{1,5},{5,9},{9,13},{13,1},{2,6},{6,10},{... | collective-permute-start | bytes 1179656 | tf_op jit(solution)/shard_map/ppermute | solution.py:1099
  321.8 50.6 %collective-permute-start.8 = (bf16[64,3072]{1,0:T(8,128)(2,1)S(1)}, bf16[64,3072]{1,0:T(8,128)(2,1)S(1)}, u32[]{:S(2)}, u32[]{:S(2)}) collective-permute-start(bf16[64,3072]{1,0:T(8,128)(2,1)S(1)} %get-tuple-element.52), channel_id=1, source_target_pairs={{0,8},{4,12},{8,0},{12,4},{1,9},{5,13},{9,1},{13,5},{2,10},{6,14},... | collective-permute-start | bytes 1179656 | tf_op jit(solution)/shard_map/ppermute | solution.py:1099
  322.0 50.4 %collective-permute-start.9 = (bf16[64,3072]{1,0:T(8,128)(2,1)S(1)}, bf16[64,3072]{1,0:T(8,128)(2,1)}, u32[]{:S(2)}, u32[]{:S(2)}) collective-permute-start(bf16[64,3072]{1,0:T(8,128)(2,1)S(1)} %get-tuple-element.53), channel_id=1, source_target_pairs={{0,12},{4,0},{8,4},{12,8},{1,13},{5,1},{9,5},{13,9},{2,14},{6,2},{... | collective-permute-start | bytes 1179656 | tf_op jit(solution)/shard_map/ppermute | solution.py:1099
  372.4 3.1 copy-start.3
  372.4 3.8 copy-start.2
